TPU v7x, 256 devices: a whole 4x4x8 slice. The times are simulated.
256 devices in a mesh: mem: 8 (over x, z_lo), tile: 32 (over z_hi, y, core).
Axes of the slice: x: 4, y: 4, z: 8 (z_hi: 4, z_lo: 2; z = z_hi * 2 + z_lo), core: 2. Of those that a mesh axis runs over, the one named last changes fastest.
Arguments:
- block_input: bfloat16 [16, 64, 256, 256], P('mem', None, 'tile'), may hold values from -36 to 36
- member_seeds: int32 [16], P('mem'), may hold values from 0 to 65520
- targets: float32 [2, 256, 256], P(None, 'tile'), may hold values from -6 to 6
- land_mask: int32 [256, 256], P('tile'), may hold values 0 or 1
- noise_weight: bfloat16 [64, 8], replicated, may hold values from -2 to 2
- conv_weight: bfloat16 [2, 9, 64, 64], replicated, may hold values from -0.25 to 0.25
- block_gain: float32 [2, 64], replicated, may hold values from 0.25 to 1.75
- head_weight: bfloat16 [2, 64], replicated, may hold values from -0.75 to 0.75
- head_gain: float32 [64], replicated, may hold values from 0.25 to 1.75
Outputs:
- energy_loss: float32 [], replicated
- predictions: float32 [16, 2, 256, 256], P('mem', None, 'tile')
- grad_conv: float32 [2, 9, 64, 64], replicated
- grad_block_gain: float32 [2, 64], replicated
- grad_head_weight: float32 [2, 64], replicated
- grad_head_gain: float32 [64], replicated
- grad_noise_weight: float32 [64, 8], replicated
Inputs may be any that keep to these rules, and one draw needn't show every extreme that they name: `member_seeds`: each member's noise seed.
All inputs are finite; a program needn't handle non-finite values. No bound on the sum of `land_mask` on one device may be relied on, other than what follows from the above.
Results may differ from a plain program's by a relative error of at most 0.0034.
The roundings to bfloat16 on the way count: a program that leaves them out, or rounds other values in their place, can miss the bound.
Values may be sent and summed in bfloat16 or wider, within the bound.
A program may use at most 64 MiB of HBM per device.

v0:
```python
import jax
import jax.numpy as jnp
from jax import lax
from jax.sharding import PartitionSpec as P

LOSS_SCALE = 16384


eps_norm = 1e-05
smooth_sq = 0.01


def extended(cells, sides, width):
    for axis, dim in sides:
        count = lax.axis_size(axis)
        ends = count - 1
        head = lax.slice_in_dim(cells, 0, width, axis=dim)
        tail = lax.slice_in_dim(cells, cells.shape[dim] - width, cells.shape[dim], axis=dim)
        cells = jnp.concatenate(
            [
                lax.ppermute(tail, axis, [(i, (i + 1) % count) for i in range(ends)]),
                cells,
                lax.ppermute(head, axis, [((i + 1) % count, i) for i in range(ends)]),
            ],
            axis=dim,
        )
    return cells


def noise_field(seed_values, row_start, row_count, col_count, total_rows, channel_count):
    grid_shape = (seed_values.shape[0], channel_count, row_count, col_count)
    channel_ids = lax.broadcasted_iota(jnp.int32, grid_shape, 1)
    row_ids = jnp.clip(
        lax.broadcasted_iota(jnp.int32, grid_shape, 2) + row_start, 0, total_rows - 1
    )
    column_ids = lax.broadcasted_iota(jnp.int32, grid_shape, 3)
    section_one = (
        seed_values[:, None, None, None] + 7919 * channel_ids + row_ids * col_count + column_ids
    ) % 65521
    section_two = (section_one * 3001 + 12345) % 65521
    folded = section_two % 46337
    section_three = (folded * folded + section_two) % 65521
    section_four = (section_three * 2897 + 4111) % 65521
    return ((section_four - 32760).astype(jnp.float32) / 18914.0).astype(jnp.bfloat16)


def rms_parts(stream):
    rms_scale = jnp.sqrt(jnp.mean(stream * stream, axis=1, keepdims=True) + eps_norm)
    return (stream / rms_scale, rms_scale)


def norm_back(normed_grad, normed, rms_scale):
    return (
        normed_grad - normed * jnp.mean(normed_grad * normed, axis=1, keepdims=True)
    ) / rms_scale


def pad_columns(bordered):
    return jnp.pad(bordered, ((0, 0), (0, 0), (0, 0), (1, 1)))


def conv_rows(padded, weights, transpose):
    row_count = padded.shape[2] - 2
    col_count = padded.shape[3] - 2
    running = None
    for offset_r in range(3):
        for offset_c in range(3):
            if transpose:
                window = padded[
                    :,
                    :,
                    2 - offset_r : 2 - offset_r + row_count,
                    2 - offset_c : 2 - offset_c + col_count,
                ]
                tap_term = jnp.einsum(
                    "oi,morw->mirw",
                    weights[3 * offset_r + offset_c],
                    window,
                    preferred_element_type=jnp.float32,
                )
            else:
                window = padded[
                    :, :, offset_r : offset_r + row_count, offset_c : offset_c + col_count
                ]
                tap_term = jnp.einsum(
                    "oi,mirw->morw",
                    weights[3 * offset_r + offset_c],
                    window,
                    preferred_element_type=jnp.float32,
                )
            running = tap_term if running is None else running + tap_term
    return running


def on_device(
    block_input,
    member_seeds,
    targets,
    land_mask,
    noise_weight,
    conv_weight,
    block_gain,
    head_weight,
    head_gain,
):
    members_here, channels, row_count, col_count = block_input.shape
    blocks = conv_weight.shape[0]
    noise_count = noise_weight.shape[1]
    total_rows = row_count * lax.axis_size("tile")
    members_all = members_here * lax.axis_size("mem")
    row_start = lax.axis_index("tile") * row_count
    stored = []
    noise_local = noise_field(
        member_seeds, row_start, row_count, col_count, total_rows, noise_count
    )
    stream = block_input.astype(jnp.float32) + jnp.einsum(
        "ck,mkrw->mcrw", noise_weight, noise_local, preferred_element_type=jnp.float32
    )
    for layer_index in range(blocks):
        normed, rms_scale = rms_parts(stream)
        inputs = (normed * block_gain[layer_index][None, :, None, None]).astype(jnp.bfloat16)
        bordered = extended(inputs, (("tile", 2),), 1)
        padded = pad_columns(bordered)
        conv_out = conv_rows(padded, conv_weight[layer_index], False)
        stored.append((normed, rms_scale, padded, conv_out))
        stream = stream + jax.nn.silu(conv_out)
    normed, rms_scale = rms_parts(stream)
    head_in = (normed * head_gain[None, :, None, None]).astype(jnp.bfloat16)
    predictions = jnp.einsum(
        "vc,mcrw->mvrw", head_weight, head_in, preferred_element_type=jnp.float32
    )
    row_float = (lax.iota(jnp.int32, row_count) + row_start).astype(jnp.float32)
    area_weight = 1.0 - 2.0 * row_float / (3.0 * total_rows)
    weight = area_weight[:, None] * (1.0 + land_mask.astype(jnp.float32))
    misfit_diff = predictions - targets[None]
    misfit = jnp.sqrt(jnp.sum(misfit_diff * misfit_diff, axis=1) + smooth_sq)
    spread_const = jnp.sqrt(jnp.float32(smooth_sq))
    cells_all = total_rows * col_count
    pairs_norm = 2.0 * members_all * (members_all - 1)
    pred_diff = predictions[:, None] - lax.all_gather(predictions, "mem", axis=0, tiled=True)[None]
    spread = jnp.sqrt(jnp.sum(pred_diff * pred_diff, axis=2) + smooth_sq)
    pair_total = jnp.sum(spread, axis=1)
    pull_sum = jnp.sum(pred_diff / spread[:, :, None], axis=1)
    pair_part = jnp.sum(weight[None] * (pair_total - spread_const))
    misfit_part = jnp.sum(weight[None] * misfit)
    loss_part = (misfit_part / members_all - pair_part / pairs_norm) / cells_all
    grad_coef = weight * (LOSS_SCALE / cells_all)
    pred_grad = (
        grad_coef[None, None]
        * (
            misfit_diff / misfit[:, None] / members_all
            - pull_sum / (members_all * (members_all - 1.0))
        )
    ).astype(jnp.bfloat16)
    grad_head_weight = jnp.einsum(
        "mvrw,mcrw->vc", pred_grad, head_in, preferred_element_type=jnp.float32
    )
    head_in_grad = jnp.einsum(
        "vc,mvrw->mcrw", head_weight, pred_grad, preferred_element_type=jnp.float32
    )
    grad_head_gain = jnp.sum(head_in_grad * normed, axis=(0, 2, 3))
    stream_grad = norm_back(head_in_grad * head_gain[None, :, None, None], normed, rms_scale)
    conv_grads = []
    gain_grads = []
    for layer_index in reversed(range(blocks)):
        normed_b, scale_b, padded_b, conv_out = stored[layer_index]
        sigmoid_out = jax.nn.sigmoid(conv_out)
        silu_slope = sigmoid_out * (1.0 + conv_out * (1.0 - sigmoid_out))
        conv_grad = (stream_grad * silu_slope).astype(jnp.bfloat16)
        bordered_grad = extended(conv_grad, (("tile", 2),), 1)
        input_grad = conv_rows(pad_columns(bordered_grad), conv_weight[layer_index], True)
        tap_grads = []
        for offset_r in range(3):
            for offset_c in range(3):
                window = padded_b[
                    :, :, offset_r : offset_r + row_count, offset_c : offset_c + col_count
                ]
                tap_grads.append(
                    jnp.einsum(
                        "morw,mirw->oi", conv_grad, window, preferred_element_type=jnp.float32
                    )
                )
        conv_grads.append(jnp.stack(tap_grads))
        gain_grads.append(jnp.sum(input_grad * normed_b, axis=(0, 2, 3)))
        stream_grad = stream_grad + norm_back(
            input_grad * block_gain[layer_index][None, :, None, None], normed_b, scale_b
        )
    entry_grad = stream_grad.astype(jnp.bfloat16)
    grad_noise_weight = jnp.einsum(
        "mcrw,mkrw->ck", entry_grad, noise_local, preferred_element_type=jnp.float32
    )
    partials = (
        loss_part,
        jnp.stack(conv_grads[::-1]),
        jnp.stack(gain_grads[::-1]),
        grad_head_weight,
        grad_head_gain,
        grad_noise_weight,
    )
    over_tiles = lax.psum(
        (partials[0], partials[1], partials[2], partials[3], partials[4], partials[5]), "tile"
    )
    totals = lax.psum(
        (over_tiles[0], over_tiles[1], over_tiles[2], over_tiles[3], over_tiles[4], over_tiles[5]),
        "mem",
    )
    return (totals[0], predictions, totals[1], totals[2], totals[3], totals[4], totals[5])


def solution(mesh):
    return jax.shard_map(
        on_device,
        mesh=mesh,
        in_specs=(
            P("mem", None, "tile", None),
            P("mem"),
            P(None, "tile", None),
            P("tile", None),
            P(),
            P(),
            P(),
            P(),
            P(),
        ),
        out_specs=(P(), P("mem", None, "tile", None), P(), P(), P(), P(), P()),
        check_vma=False,
    )
```

profile of v0, /device:TPU:1, one launch (start us, length us, event | category | flops | bytes accessed | tf_op | source)
XLA Modules:
  0.0 491.0 jit_solution(5551400707822578918)
XLA Ops:
  7.3 0.8 slice_bitcast_fusion
  8.0 1.7 multiply_reduce_fusion.8
  10.1 4.7 collective-permute-start
  14.9 1.9 collective-permute-start.1
  16.8 3.6 collective-permute-done.1
  20.4 0.5 select_maximum_fusion.6
  21.0 0.4 fusion.76
  21.9 0.4 convolution_add_fusion.12
  22.9 0.4 convolution_add_fusion.9
  23.5 1.6 multiply_reduce_fusion.7
  25.4 1.9 collective-permute-start.2
  27.4 2.4 collective-permute-start.3
  29.9 3.1 collective-permute-done.3
  32.9 0.5 select_maximum_fusion.4
  33.5 0.4 fusion.63
  34.4 0.4 convolution_add_fusion.5
  35.3 0.4 convolution_add_fusion.2
  36.0 0.6 multiply_reduce_fusion.6
  37.5 23.2 %all_gather.3 = f32[16,2,8,256]{3,2,1,0:T(8,128)S(1)} all-gather(f32[2,2,8,256]{3,2,1,0:T(8,128)S(1)} %copy.64), channel_id=1, replica_groups=mesh['mem'=8,'tile'=32] {'mem'}, dimensions={0}, use_global_device_ids=true | all-gather | bytes 294912 | tf_op jit(solution)/shard_map/all_gather | solution.py:140
  61.0 0.6 multiply_reduce_fusion.10
  61.6 0.5 multiply_reduce_fusion.1
  62.1 0.6 multiply_convert_fusion.1
  62.7 0.4 copy-done.3
  63.1 0.6 fusion.220
  64.0 7.6 %collective-permute-start.4 = (bf16[2,64,1,256]{3,1,2,0:T(8,128)(2,1)}, bf16[2,64,1,256]{3,1,2,0:T(8,128)(2,1)}, u32[]{:S(2)}, u32[]{:S(2)}) collective-permute-start(bf16[2,64,1,256]{3,1,2,0:T(8,128)(2,1)} %get-tuple-element.54), channel_id=1, source_target_pairs={{0,1},{1,2},{2,3},{3,4},{4,5},{5,6},{6,7},{7,8},{8,9},{9,10},{10,1... | collective-permute-start | bytes 196616 | tf_op jit(solution)/shard_map/ppermute | solution.py:21
  71.7 2.1 collective-permute-start.5
  74.1 0.4 fusion.18
  75.1 0.4 fusion.15
  76.0 0.4 fusion.12
  76.7 0.4 copy-done.10
  78.5 1.4 select_maximum_fusion.2
  79.9 0.3 fusion.55
  80.2 1.2 fusion.30
  81.4 0.4 convolution_add_fusion.25
  81.8 0.3 convolution_add_fusion.24
  82.2 0.4 convolution_add_fusion.23
  82.6 0.3 convolution_add_fusion.22
  83.3 1.3 fusion.34
  84.6 0.8 multiply_reduce_fusion.2
  85.4 0.4 copy-done.4
  86.1 1.9 multiply_convert_fusion
  88.4 3.6 collective-permute-start.6
  92.0 1.9 collective-permute-start.7
  94.2 0.4 fusion.27
  95.2 0.4 fusion.24
  96.3 0.4 fusion.21
  97.0 0.9 pad_maximum_fusion
  97.9 0.5 select_maximum_fusion
  98.5 0.3 fusion.48
  98.8 0.3 fusion.38
  99.2 0.4 convolution_add_fusion.19
  99.6 0.3 convolution_add_fusion.18
  99.9 0.4 convolution_add_fusion.17
  100.3 0.3 convolution_add_fusion.16
  100.7 0.3 convolution_add_fusion.15
  101.1 0.5 copy-done.13
  101.5 0.3 fusion.42
  101.9 0.9 copy-done.6
  102.8 1.8 multiply_reduce_fusion
  104.6 285.0 %all-reduce.9.cloned.1.call-done = f32[2,9,64,64]{3,2,1,0:T(8,128)} async-done(((f32[2,9,64,64]{3,2,1,0:T(8,128)}), f32[2,9,64,64]{3,2,1,0:T(8,128)}) %all-reduce.9.cloned.1.call-update) | async-done | bytes 294928 | tf_op jit(solution)/shard_map/psum | solution.py:200
  389.6 2.4 convolution_bitcast_fusion.21
  392.0 73.7 %all-reduce.4 = (f32[]{:T(128)}, f32[2,64]{1,0:T(2,128)S(1)}, f32[2,64]{1,0:T(2,128)S(1)}, f32[64]{0:T(128)S(1)}, f32[64,8]{0,1:T(8,128)S(1)}) all-reduce(f32[]{:T(128)S(6)} %div.134, f32[2,64]{1,0:T(2,128)S(1)} %pad_maximum_fusion.13, f32[2,64]{1,0:T(2,128)S(1)} %convolution_bitcast_fusion.22, ...), channel_id=1, replica_groups=mesh['mem'=8,'tile'=32] {'tile'}, use_global_device_ids=true, to_apply=%region_8.9 | all-reduce | flops 833 | bytes 6664 | tf_op jit(solution)/shard_map/psum | solution.py:200
  465.7 16.6 %all-reduce.5 = (f32[]{:T(128)}, f32[2,64]{1,0:T(2,128)}, f32[2,64]{1,0:T(2,128)}, f32[64]{0:T(128)}, f32[64,8]{0,1:T(8,128)}) all-reduce(f32[]{:T(128)} %get-tuple-element.36, f32[2,64]{1,0:T(2,128)S(1)} %get-tuple-element.37, f32[2,64]{1,0:T(2,128)S(1)} %get-tuple-element.38, ...), channel_id=1, replica_groups=mesh['mem'=8,'tile'=32] {'mem'}, use_global_device_ids=true, to_apply=%region_9.10 | all-reduce | flops 833 | bytes 6664 | tf_op jit(solution)/shard_map/psum | solution.py:203
  482.3 1.9 copy.192
  (98 shorter events, 9.7 us)
Async XLA Ops:
  7.2 0.9 copy-start
  7.2 382.4 %all-reduce.9.cloned.1.call-start = ((), (), s32[]{:S(2)}) async-start(), calls=%async_computation | async-start | bytes 1179648 | tf_op jit(solution)/shard_map/psum | solution.py:200
  7.2 2.5 copy-start.21
  9.8 13.8 %copy-start.5 = (f32[2,64,8,256]{3,1,2,0:T(8,128)}, f32[2,64,8,256]{3,1,2,0:T(8,128)S(1)}, u32[]{:S(2)}) copy-start(f32[2,64,8,256]{3,1,2,0:T(8,128)S(1)} %get-tuple-element.66) | copy-start | bytes 3145732
  10.1 10.9 %copy-start.8 = (bf16[2,9,64,64]{3,2,1,0:T(8,128)(2,1)S(1)}, bf16[2,9,64,64]{3,2,1,0:T(8,128)(2,1)}, u32[]{:S(2)}) copy-start(bf16[2,9,64,64]{3,2,1,0:T(8,128)(2,1)} %param.14) | copy-start | bytes 442372
  10.1 6.7 %collective-permute-start = (bf16[2,64,1,256]{3,1,2,0:T(8,128)(2,1)S(1)}, bf16[2,64,1,256]{3,1,2,0:T(8,128)(2,1)S(1)}, u32[]{:S(2)}, u32[]{:S(2)}) collective-permute-start(bf16[2,64,1,256]{3,1,2,0:T(8,128)(2,1)S(1)} %get-tuple-element.58), channel_id=1, source_target_pairs={{0,1},{1,2},{2,3},{3,4},{4,5},{5,6},{6,7},{7,8},{8,9},{9,10},{10,1... | collective-permute-start | bytes 196616 | tf_op jit(solution)/shard_map/ppermute | solution.py:21
  14.9 5.6 %collective-permute-start.1 = (bf16[2,64,1,256]{3,1,2,0:T(8,128)(2,1)S(1)}, bf16[2,64,1,256]{3,1,2,0:T(8,128)(2,1)S(1)}, u32[]{:S(2)}, u32[]{:S(2)}) collective-permute-start(bf16[2,64,1,256]{3,1,2,0:T(8,128)(2,1)S(1)} %get-tuple-element.59), channel_id=1, source_target_pairs={{1,0},{2,1},{3,2},{4,3},{5,4},{6,5},{7,6},{8,7},{9,8},{10,9},{11,1... | collective-permute-start | bytes 196616 | tf_op jit(solution)/shard_map/ppermute | solution.py:23
  20.4 3.1 copy-start.14
  25.1 11.5 %copy-start.1 = (f32[2,64,8,256]{3,1,2,0:T(8,128)}, f32[2,64,8,256]{3,1,2,0:T(8,128)S(1)}, u32[]{:S(2)}) copy-start(f32[2,64,8,256]{3,1,2,0:T(8,128)S(1)} %get-tuple-element.51) | copy-start | bytes 3145732
  25.1 4.7 copy-start.18
  25.1 4.8 copy-start.16
  25.4 4.4 collective-permute-start.2
  27.4 5.6 %collective-permute-start.3 = (bf16[2,64,1,256]{3,1,2,0:T(8,128)(2,1)S(1)}, bf16[2,64,1,256]{3,1,2,0:T(8,128)(2,1)S(1)}, u32[]{:S(2)}, u32[]{:S(2)}) collective-permute-start(bf16[2,64,1,256]{3,1,2,0:T(8,128)(2,1)S(1)} %get-tuple-element.57), channel_id=1, source_target_pairs={{1,0},{2,1},{3,2},{4,3},{5,4},{6,5},{7,6},{8,7},{9,8},{10,9},{11,1... | collective-permute-start | bytes 196616 | tf_op jit(solution)/shard_map/ppermute | solution.py:23
  36.6 0.7 copy-start.17
  36.6 0.7 copy-start.19
  37.5 24.6 %copy-start.9 = (f32[2,2,8,256]{3,2,1,0:T(8,128)}, f32[2,2,8,256]{3,2,1,0:T(8,128)S(1)}, u32[]{:S(2)}) copy-start(f32[2,2,8,256]{3,2,1,0:T(8,128)S(1)} %copy.64) | copy-start | bytes 98308
  62.1 1.0 copy-start.3
  64.0 14.4 %collective-permute-start.4 = (bf16[2,64,1,256]{3,1,2,0:T(8,128)(2,1)}, bf16[2,64,1,256]{3,1,2,0:T(8,128)(2,1)}, u32[]{:S(2)}, u32[]{:S(2)}) collective-permute-start(bf16[2,64,1,256]{3,1,2,0:T(8,128)(2,1)} %get-tuple-element.54), channel_id=1, source_target_pairs={{0,1},{1,2},{2,3},{3,4},{4,5},{5,6},{6,7},{7,8},{8,9},{9,10},{10,1... | collective-permute-start | bytes 196616 | tf_op jit(solution)/shard_map/ppermute | solution.py:21
  71.7 6.8 %collective-permute-start.5 = (bf16[2,64,1,256]{3,1,2,0:T(8,128)(2,1)}, bf16[2,64,1,256]{3,1,2,0:T(8,128)(2,1)}, u32[]{:S(2)}, u32[]{:S(2)}) collective-permute-start(bf16[2,64,1,256]{3,1,2,0:T(8,128)(2,1)} %get-tuple-element.55), channel_id=1, source_target_pairs={{1,0},{2,1},{3,2},{4,3},{5,4},{6,5},{7,6},{8,7},{9,8},{10,9},{11,1... | collective-permute-start | bytes 196616 | tf_op jit(solution)/shard_map/ppermute | solution.py:23
  76.4 0.7 copy-start.10
  83.3 1.3 copy-start.2
  84.6 1.2 copy-start.4
  84.6 1.5 copy-start.7
  88.4 9.5 %collective-permute-start.6 = (bf16[2,64,1,256]{3,1,2,0:T(8,128)(2,1)S(1)}, bf16[2,64,1,256]{3,1,2,0:T(8,128)(2,1)S(1)}, u32[]{:S(2)}, u32[]{:S(2)}) collective-permute-start(bf16[2,64,1,256]{3,1,2,0:T(8,128)(2,1)S(1)} %get-tuple-element.52), channel_id=1, source_target_pairs={{0,1},{1,2},{2,3},{3,4},{4,5},{5,6},{6,7},{7,8},{8,9},{9,10},{10,1... | collective-permute-start | bytes 196616 | tf_op jit(solution)/shard_map/ppermute | solution.py:21
  92.0 5.9 %collective-permute-start.7 = (bf16[2,64,1,256]{3,1,2,0:T(8,128)(2,1)S(1)}, bf16[2,64,1,256]{3,1,2,0:T(8,128)(2,1)S(1)}, u32[]{:S(2)}, u32[]{:S(2)}) collective-permute-start(bf16[2,64,1,256]{3,1,2,0:T(8,128)(2,1)S(1)} %get-tuple-element.53), channel_id=1, source_target_pairs={{1,0},{2,1},{3,2},{4,3},{5,4},{6,5},{7,6},{8,7},{9,8},{10,9},{11,1... | collective-permute-start | bytes 196616 | tf_op jit(solution)/shard_map/ppermute | solution.py:23
  95.2 0.8 copy-start.15
  96.0 1.0 copy-start.11
  97.9 384.4 %all-reduce.11.cloned.1.call-start = ((), (), s32[]{:S(2)}) async-start(), calls=%async_computation.1 | async-start | bytes 1179648 | tf_op jit(solution)/shard_map/psum | solution.py:203
  97.9 0.9 copy-start.12
  100.7 0.8 copy-start.13
  101.5 1.2 copy-start.6
  102.8 286.8 %copy-start.20 = (s32[2]{0:T(128)S(1)}, s32[2]{0:T(128)}, u32[]{:S(2)}) copy-start(s32[2]{0:T(128)} %param.10) | copy-start | bytes 28
  102.8 286.8 %copy-start.22 = (s32[8]{0:T(128)S(1)}, s32[8]{0:T(128)}, u32[]{:S(2)}) copy-start(s32[8]{0:T(128)} %copy-done.21) | copy-start | bytes 100
Sparse Core Ops, SparseCore 0:
  98.0 291.5 all-reduce.8
  392.4 76.5 all-reduce.10
where the time goes:
time: 495 us; the launch traced here: 491 us
  waiting for transfers between devices  292 us (59%)
  blocking collectives  113 us (23%)
  matrix products  28 us (6%)
  starting transfers between devices  26.3 us (5%)
  between operations  16.2 us (3%)
  other arithmetic  8.17 us (2%)
  local copies, waits for them, and re-layouts  7.12 us (1%)
    psum x1, waiting for transfers between devices, on_device(): lax.psum((partials[0], partials[1], partials[2], partials[3], partials[4]...  285 us
    psum x1, blocking collectives, on_device(): lax.psum((partials[0], partials[1], partials[2], partials[3], partials[4]...  73.7 us
    all_gather x1, blocking collectives, on_device(): lax.all_gather(predictions, 'mem', axis=0, tiled=True)[None]  23.2 us
    ppermute x4, starting transfers between devices, extended(): lax.ppermute(tail, axis, [(i, (i + 1) % count) for i in range(ends)])  17.9 us
    psum x1, blocking collectives, on_device(): lax.psum((over_tiles[0], over_tiles[1], over_tiles[2], over_tiles[3], ove...  16.6 us
    dot_general x18, matrix products, conv_rows(): jnp.einsum('oi,morw->mirw', weights[3 * offset_r + offset_c], window, pre...  10.1 us
  transfers between devices with their start and end apart: 10, of which 3 were waited for; matrix products, arithmetic and copies ran while one was open for 3% of the time, Pallas kernels for 0%

commit v1 on v0

--- a/solution.py
+++ b/solution.py
@@ -1,11 +1,15 @@
 import jax
 import jax.numpy as jnp
 from jax import lax
+from jax.experimental import pallas as pl
+from jax.experimental.pallas import tpu as pltpu
 from jax.sharding import PartitionSpec as P
 
 LOSS_SCALE = 16384
 
 
+MESH_ID = pl.DeviceIdType.MESH
+GROUP = 16
 eps_norm = 1e-05
 smooth_sq = 0.01
 
@@ -25,6 +29,156 @@
             axis=dim,
         )
     return cells
+
+
+def coordinates():
+    mem, tile = lax.axis_index("mem"), lax.axis_index("tile")
+    return mem // 2, (tile // 2) % 4, (tile // 8) * 2 + mem % 2, tile % 2
+
+
+def device_at(x, y, z, core):
+    return (x * 2 + z % 2, (z // 2) * 8 + y * 2 + core)
+
+
+def plane_rank():
+    x, y, _, _ = coordinates()
+    return x * 4 + y
+
+
+def plane_device(rank):
+    _, _, z, core = coordinates()
+    return device_at(rank // 4, rank % 4, z, core)
+
+
+def line_rank():
+    _, _, z, core = coordinates()
+    return z * 2 + core
+
+
+def line_device(rank):
+    x, y, _, _ = coordinates()
+    return device_at(x, y, rank // 2, rank % 2)
+
+
+def others(rank):
+    return [lax.rem(rank + step, GROUP) for step in range(1, GROUP)]
+
+
+def sum_kernel(parts, out, mine, scattered, spread, plane_sems, line_sems, back_sems):
+    in_plane, in_line = plane_rank(), line_rank()
+    barrier = pltpu.get_barrier_semaphore()
+    for rank in others(in_plane):
+        pl.semaphore_signal(barrier, inc=1, device_id=plane_device(rank), device_id_type=MESH_ID)
+    for rank in others(in_line):
+        pl.semaphore_signal(barrier, inc=1, device_id=line_device(rank), device_id_type=MESH_ID)
+    pl.semaphore_wait(barrier, 2 * (GROUP - 1))
+
+    def exchange(ranks, device, source, target, sems):
+        copies = []
+        for step, rank in enumerate(ranks):
+            copy = pltpu.make_async_remote_copy(
+                src_ref=source(rank),
+                dst_ref=target(step),
+                send_sem=sems.at[0, step],
+                recv_sem=sems.at[1, step],
+                device_id=device(rank),
+                device_id_type=MESH_ID,
+            )
+            copy.start()
+            copies.append(copy)
+        for copy in copies:
+            copy.wait()
+
+    exchange(
+        others(in_plane),
+        plane_device,
+        lambda rank: parts.at[rank],
+        lambda step: scattered.at[step],
+        plane_sems,
+    )
+    total = parts[in_plane]
+    for step in range(GROUP - 1):
+        total = total + scattered[step]
+    spread[in_line] = total
+    exchange(
+        others(in_line),
+        line_device,
+        lambda rank: spread.at[in_line],
+        lambda step: spread.at[in_line],
+        line_sems,
+    )
+    total = spread[0]
+    for rank in range(1, GROUP):
+        total = total + spread[rank]
+    out[in_plane] = total
+    exchange(
+        others(in_plane),
+        plane_device,
+        lambda rank: out.at[in_plane],
+        lambda step: out.at[in_plane],
+        back_sems,
+    )
+
+
+def sum_everywhere(parts):
+    rows = parts.shape[1]
+    return pl.pallas_call(
+        sum_kernel,
+        out_shape=jax.ShapeDtypeStruct(parts.shape, jnp.float32),
+        in_specs=[pl.BlockSpec(memory_space=pltpu.VMEM)],
+        out_specs=pl.BlockSpec(memory_space=pltpu.VMEM),
+        scratch_shapes=[
+            pltpu.VMEM((rows, 128), jnp.float32),
+            pltpu.VMEM((GROUP - 1, rows, 128), jnp.float32),
+            pltpu.VMEM((GROUP, rows, 128), jnp.float32),
+            pltpu.SemaphoreType.DMA((2, GROUP - 1)),
+            pltpu.SemaphoreType.DMA((2, GROUP - 1)),
+            pltpu.SemaphoreType.DMA((2, GROUP - 1)),
+        ],
+        compiler_params=pltpu.CompilerParams(
+            collective_id=0, has_side_effects=True, vmem_limit_bytes=32 * 2**20
+        ),
+        name="sum_everywhere",
+    )(parts)
+
+
+def gather_kernel(own, out, send_sems, recv_sems):
+    mem = lax.axis_index("mem")
+    tile = lax.axis_index("tile")
+    barrier = pltpu.get_barrier_semaphore()
+    ranks = [lax.rem(mem + step, 8) for step in range(1, 8)]
+    for rank in ranks:
+        pl.semaphore_signal(barrier, inc=1, device_id=(rank, tile), device_id_type=MESH_ID)
+    pl.semaphore_wait(barrier, 7)
+    out[mem] = own[...]
+    copies = []
+    for step, rank in enumerate(ranks):
+        copy = pltpu.make_async_remote_copy(
+            src_ref=own,
+            dst_ref=out.at[mem],
+            send_sem=send_sems.at[step],
+            recv_sem=recv_sems.at[step],
+            device_id=(rank, tile),
+            device_id_type=MESH_ID,
+        )
+        copy.start()
+        copies.append(copy)
+    for copy in copies:
+        copy.wait()
+
+
+def gather_members(own):
+    return pl.pallas_call(
+        gather_kernel,
+        out_shape=jax.ShapeDtypeStruct((8,) + own.shape, jnp.float32),
+        in_specs=[pl.BlockSpec(memory_space=pltpu.VMEM)],
+        out_specs=pl.BlockSpec(memory_space=pltpu.VMEM),
+        scratch_shapes=[pltpu.SemaphoreType.DMA((7,)), pltpu.SemaphoreType.DMA((7,))],
+        compiler_params=pltpu.CompilerParams(
+            collective_id=1, has_side_effects=True, vmem_limit_bytes=32 * 2**20
+        ),
+        name="gather_members",
+    )(own)
 
 
 def noise_field(seed_values, row_start, row_count, col_count, total_rows, channel_count):
@@ -137,7 +291,7 @@
     spread_const = jnp.sqrt(jnp.float32(smooth_sq))
     cells_all = total_rows * col_count
     pairs_norm = 2.0 * members_all * (members_all - 1)
-    pred_diff = predictions[:, None] - lax.all_gather(predictions, "mem", axis=0, tiled=True)[None]
+    pred_diff = predictions[:, None] - gather_members(predictions).reshape((members_all,) + predictions.shape[1:])[None]
     spread = jnp.sqrt(jnp.sum(pred_diff * pred_diff, axis=2) + smooth_sq)
     pair_total = jnp.sum(spread, axis=1)
     pull_sum = jnp.sum(pred_diff / spread[:, :, None], axis=1)
@@ -197,13 +351,14 @@
         grad_head_gain,
         grad_noise_weight,
     )
-    over_tiles = lax.psum(
-        (partials[0], partials[1], partials[2], partials[3], partials[4], partials[5]), "tile"
-    )
-    totals = lax.psum(
-        (over_tiles[0], over_tiles[1], over_tiles[2], over_tiles[3], over_tiles[4], over_tiles[5]),
-        "mem",
-    )
+    flat = jnp.concatenate([part.reshape(-1) for part in partials])
+    rows = -(-flat.size // (GROUP * 1024)) * 8
+    packed = jnp.pad(flat, (0, GROUP * rows * 128 - flat.size)).reshape(GROUP, rows, 128)
+    summed = sum_everywhere(packed).reshape(-1)
+    totals, at = [], 0
+    for part in partials:
+        totals.append(summed[at : at + part.size].reshape(part.shape))
+        at += part.size
     return (totals[0], predictions, totals[1], totals[2], totals[3], totals[4], totals[5])
 
 

time: 495 us -> 136 us (0.27)
  waiting for transfers between devices: 292 us -> 7.22 us
  blocking collectives: 113 us -> 0 us
  Pallas kernels: 0 us -> 54.5 us
  between operations: 16.2 us -> 2.81 us
  local copies, waits for them, and re-layouts: 7.12 us -> 13.2 us
    psum x2 -> x0, waiting for transfers between devices: 285 us -> none  [the longest x1 285 us: on_device(): lax.psum((partials[0], partials[1], partials[2], partials[3], partials[4]...]
    psum x2 -> x0, blocking collectives: 90.3 us -> none  [the longest x1 73.7 us: on_device(): lax.psum((partials[0], partials[1], partials[2], partials[3], partials[4]...]
    pallas_call x0 -> x2, Pallas kernels: none -> 54.5 us  [the longest x1 46.8 us: sum_everywhere(): pl.pallas_call(sum_kernel, out_shape=jax.ShapeDtypeStruct(parts.shape, jn...]
    all_gather x1 -> x0, blocking collectives: 23.2 us -> none  [on_device(): lax.all_gather(predictions, 'mem', axis=0, tiled=True)[None]]
  transfers between devices with their start and end apart: 10 -> 8, of which waited for: 3 -> 3; matrix products, arithmetic and copies ran while one was open for 3% -> 4% of each run, Pallas kernels for 0% -> 0%
where the time goes in v1:
time: 136 us; the launch traced here: 135 us
  Pallas kernels  54.5 us (40%)
  matrix products  26.2 us (19%)
  starting transfers between devices  23.2 us (17%)
  local copies, waits for them, and re-layouts  13.2 us (10%)
  other arithmetic  8.19 us (6%)
  waiting for transfers between devices  7.22 us (5%)
  between operations  2.81 us (2%)
    pallas_call x1, Pallas kernels, sum_everywhere(): pl.pallas_call(sum_kernel, out_shape=jax.ShapeDtypeStruct(parts.shape, jn...  46.8 us
    ppermute x4, starting transfers between devices, extended(): lax.ppermute(tail, axis, [(i, (i + 1) % count) for i in range(ends)])  14.6 us
    dot_general x18, matrix products, conv_rows(): jnp.einsum('oi,morw->mirw', weights[3 * offset_r + offset_c], window, pre...  9.95 us
    ppermute x4, starting transfers between devices, extended(): lax.ppermute(head, axis, [((i + 1) % count, i) for i in range(ends)])  8.57 us
    pallas_call x1, Pallas kernels, gather_members(): pl.pallas_call(gather_kernel, out_shape=jax.ShapeDtypeStruct((8,) + own.s...  7.69 us
    ppermute x4, waiting for transfers between devices, extended(): lax.ppermute(head, axis, [((i + 1) % count, i) for i in range(ends)])  7.21 us
    dot_general x18, matrix products, conv_rows(): jnp.einsum('oi,mirw->morw', weights[3 * offset_r + offset_c], window, pre...  7.07 us
    dot_general x18, matrix products, on_device(): jnp.einsum('morw,mirw->oi', conv_grad, window, preferred_element_type=jnp...  5.59 us
  transfers between devices with their start and end apart: 8, of which 3 were waited for; matrix products, arithmetic and copies ran while one was open for 4% of the time, Pallas kernels for 0%

profile of v1, /device:TPU:1, one launch (start us, length us, event | category | flops | bytes accessed | tf_op | source)
XLA Modules:
  0.0 135.4 jit_solution(10372439187365454174)
XLA Ops:
  0.7 0.8 slice_bitcast_fusion
  1.4 1.7 %multiply_reduce_fusion.8 = (f32[2,8,256]{2,1,0:T(8,128)S(1)}, f32[2,64,8,256]{3,1,2,0:T(8,128)S(1)}) fusion(bf16[64,8]{0,1:T(8,128)(2,1)S(1)} %copy-done, s32[8]{0:T(128)S(1)} %get-tuple-element.60, s32[8]{0:T(128)S(1)} %get-tuple-element.61, s32[2]{0:T(128)} %param.10, bf16[2,64,8,256]{3,2,1,0:T(8,128)(2,1)} %param.9), kind=kOutput, calls=%fused_computation.100 | convolution fusion | flops 6647808 | bytes 1590344 | tf_op jit(solution)/shard_map/ck,mkrw->mcrw/dot_general | solution.py:270
  3.5 4.7 %collective-permute-start = (bf16[2,64,1,256]{3,1,2,0:T(8,128)(2,1)S(1)}, bf16[2,64,1,256]{3,1,2,0:T(8,128)(2,1)S(1)}, u32[]{:S(2)}, u32[]{:S(2)}) collective-permute-start(bf16[2,64,1,256]{3,1,2,0:T(8,128)(2,1)S(1)} %get-tuple-element.43), channel_id=1, source_target_pairs={{0,1},{1,2},{2,3},{3,4},{4,5},{5,6},{6,7},{7,8},{8,9},{9,10},{10,1... | collective-permute-start | bytes 196616 | tf_op jit(solution)/shard_map/ppermute | solution.py:25
  8.3 1.9 %collective-permute-start.1 = (bf16[2,64,1,256]{3,1,2,0:T(8,128)(2,1)S(1)}, bf16[2,64,1,256]{3,1,2,0:T(8,128)(2,1)S(1)}, u32[]{:S(2)}, u32[]{:S(2)}) collective-permute-start(bf16[2,64,1,256]{3,1,2,0:T(8,128)(2,1)S(1)} %get-tuple-element.44), channel_id=1, source_target_pairs={{1,0},{2,1},{3,2},{4,3},{5,4},{6,5},{7,6},{8,7},{9,8},{10,9},{11,1... | collective-permute-start | bytes 196616 | tf_op jit(solution)/shard_map/ppermute | solution.py:27
  10.2 3.6 %collective-permute-done.1 = bf16[2,64,1,256]{3,1,2,0:T(8,128)(2,1)S(1)} collective-permute-done((bf16[2,64,1,256]{3,1,2,0:T(8,128)(2,1)S(1)}, bf16[2,64,1,256]{3,1,2,0:T(8,128)(2,1)S(1)}, u32[]{:S(2)}, u32[]{:S(2)}) %collective-permute-start.1) | collective-permute-done | bytes 65568 | tf_op jit(solution)/shard_map/ppermute | solution.py:27
  13.9 0.5 select_maximum_fusion.6
  14.4 0.4 fusion.76
  15.3 0.4 convolution_add_fusion.12
  16.3 0.4 convolution_add_fusion.9
  16.9 1.5 %multiply_reduce_fusion.7 = (f32[2,8,256]{2,1,0:T(8,128)S(1)}, f32[2,64,8,256]{3,1,2,0:T(8,128)S(1)}, f32[2,64,8,256]{3,1,2,0:T(8,128)}) fusion(f32[2,64,8,256]{3,1,2,0:T(8,128)S(1)} %get-tuple-element.53, f32[2,8,256,64]{2,3,1,0:T(8,128)S(1)} %fusion.76, f32[2,8,256,64]{2,3,1,0:T(8,128)S(1)} %convolution_add_fusion.8, ...), kind=kOutput, calls=%fused_computation.96 | convolution fusion | flops 36958208 | bytes 5865472 | tf_op jit(solution)/shard_map/oi,mirw->morw/dot_general | solution.py:239
  18.8 1.9 %collective-permute-start.2 = (bf16[2,64,1,256]{3,1,2,0:T(8,128)(2,1)S(1)}, bf16[2,64,1,256]{3,1,2,0:T(8,128)(2,1)S(1)}, u32[]{:S(2)}, u32[]{:S(2)}) collective-permute-start(bf16[2,64,1,256]{3,1,2,0:T(8,128)(2,1)S(1)} %get-tuple-element.41), channel_id=1, source_target_pairs={{0,1},{1,2},{2,3},{3,4},{4,5},{5,6},{6,7},{7,8},{8,9},{9,10},{10,1... | collective-permute-start | bytes 196616 | tf_op jit(solution)/shard_map/ppermute | solution.py:25
  20.7 2.4 %collective-permute-start.3 = (bf16[2,64,1,256]{3,1,2,0:T(8,128)(2,1)S(1)}, bf16[2,64,1,256]{3,1,2,0:T(8,128)(2,1)S(1)}, u32[]{:S(2)}, u32[]{:S(2)}) collective-permute-start(bf16[2,64,1,256]{3,1,2,0:T(8,128)(2,1)S(1)} %get-tuple-element.42), channel_id=1, source_target_pairs={{1,0},{2,1},{3,2},{4,3},{5,4},{6,5},{7,6},{8,7},{9,8},{10,9},{11,1... | collective-permute-start | bytes 196616 | tf_op jit(solution)/shard_map/ppermute | solution.py:27
  23.2 3.1 %collective-permute-done.3 = bf16[2,64,1,256]{3,1,2,0:T(8,128)(2,1)S(1)} collective-permute-done((bf16[2,64,1,256]{3,1,2,0:T(8,128)(2,1)S(1)}, bf16[2,64,1,256]{3,1,2,0:T(8,128)(2,1)S(1)}, u32[]{:S(2)}, u32[]{:S(2)}) %collective-permute-start.3) | collective-permute-done | bytes 65568 | tf_op jit(solution)/shard_map/ppermute | solution.py:27
  26.3 0.5 select_maximum_fusion.4
  26.8 0.4 fusion.63
  27.8 0.4 convolution_add_fusion.5
  28.7 0.4 convolution_add_fusion.2
  29.4 0.6 multiply_reduce_fusion.6
  30.9 0.5 copy-done.15
  31.4 7.7 %gather_members.1 = f32[8,2,2,8,256]{4,3,2,1,0:T(8,128)S(1)} custom-call(f32[2,2,8,256]{3,2,1,0:T(8,128)S(1)} %get-tuple-element.34.own), custom_call_target="tpu_custom_call" | custom-call | tf_op jit(solution)/shard_map/gather_members/pallas_call | solution.py:171
  39.3 0.6 multiply_reduce_fusion.10
  40.0 0.5 multiply_reduce_fusion.1
  40.5 0.6 multiply_convert_fusion.1
  41.1 0.4 copy-done.4
  41.5 0.7 fusion.218
  42.4 4.3 %collective-permute-start.4 = (bf16[2,64,1,256]{3,1,2,0:T(8,128)(2,1)}, bf16[2,64,1,256]{3,1,2,0:T(8,128)(2,1)}, u32[]{:S(2)}, u32[]{:S(2)}) collective-permute-start(bf16[2,64,1,256]{3,1,2,0:T(8,128)(2,1)} %get-tuple-element.39), channel_id=1, source_target_pairs={{0,1},{1,2},{2,3},{3,4},{4,5},{5,6},{6,7},{7,8},{8,9},{9,10},{10,1... | collective-permute-start | bytes 196616 | tf_op jit(solution)/shard_map/ppermute | solution.py:25
  46.8 2.1 %collective-permute-start.5 = (bf16[2,64,1,256]{3,1,2,0:T(8,128)(2,1)}, bf16[2,64,1,256]{3,1,2,0:T(8,128)(2,1)}, u32[]{:S(2)}, u32[]{:S(2)}) collective-permute-start(bf16[2,64,1,256]{3,1,2,0:T(8,128)(2,1)} %get-tuple-element.40), channel_id=1, source_target_pairs={{1,0},{2,1},{3,2},{4,3},{5,4},{6,5},{7,6},{8,7},{9,8},{10,9},{11,1... | collective-permute-start | bytes 196616 | tf_op jit(solution)/shard_map/ppermute | solution.py:27
  49.2 0.4 fusion.18
  50.2 0.4 fusion.15
  51.1 0.4 fusion.12
  51.5 0.7 copy-done.11
  53.9 1.4 %select_maximum_fusion.2 = bf16[2,64,10,258]{3,1,2,0:T(8,128)(2,1)S(1)} fusion(bf16[2,64,1,256]{3,1,2,0:T(8,128)(2,1)} %collective-permute-done.5, bf16[2,64,8,256]{3,1,2,0:T(8,128)(2,1)S(1)} %multiply_convert_fusion.1, bf16[2,64,1,256]{3,1,2,0:T(8,128)(2,1)} %collective-permute-done.4), kind=kLoop, calls=%fused_computation.103 | loop fusion | flops 3962880 | bytes 1315840 | tf_op jit(solution)/shard_map/concatenate | solution.py:23
  55.7 1.2 fusion.30
  56.9 0.4 convolution_add_fusion.25
  57.3 0.3 convolution_add_fusion.24
  57.7 0.4 convolution_add_fusion.23
  58.8 1.3 fusion.34
  60.1 0.8 multiply_reduce_fusion.2
  60.9 0.4 copy-done.5
  61.6 1.9 %multiply_convert_fusion = (bf16[2,64,8,256]{3,1,2,0:T(8,128)(2,1)S(1)}, f32[2,64,8,256]{3,1,2,0:T(8,128)}) fusion(f32[2,64,8,256]{3,1,2,0:T(8,128)S(1)} %copy-done.8, f32[2,8,256]{2,1,0:T(8,128)S(1)} %broadcast_multiply_fusion.1, f32[2,64,8,256]{3,1,2,0:T(8,128)S(1)} %copy-done.3, f32[2,8,256]{2,1,0:T(8,128)S(1)} %add_sqrt_fusion.3, ...), kind=kLoop, calls=%fused_computation.85 | loop fusion | flops 4980736 | bytes 6881792 | tf_op jit(solution)/shard_map/convert_element_type | solution.py:323
  63.5 0.7 fusion.217
  64.5 3.6 %collective-permute-start.6 = (bf16[2,64,1,256]{3,1,2,0:T(8,128)(2,1)}, bf16[2,64,1,256]{3,1,2,0:T(8,128)(2,1)S(1)}, u32[]{:S(2)}, u32[]{:S(2)}) collective-permute-start(bf16[2,64,1,256]{3,1,2,0:T(8,128)(2,1)} %get-tuple-element.37), channel_id=1, source_target_pairs={{0,1},{1,2},{2,3},{3,4},{4,5},{5,6},{6,7},{7,8},{8,9},{9,10},{10,1... | collective-permute-start | bytes 196616 | tf_op jit(solution)/shard_map/ppermute | solution.py:25
  68.1 2.1 %collective-permute-start.7 = (bf16[2,64,1,256]{3,1,2,0:T(8,128)(2,1)}, bf16[2,64,1,256]{3,1,2,0:T(8,128)(2,1)}, u32[]{:S(2)}, u32[]{:S(2)}) collective-permute-start(bf16[2,64,1,256]{3,1,2,0:T(8,128)(2,1)} %get-tuple-element.38), channel_id=1, source_target_pairs={{1,0},{2,1},{3,2},{4,3},{5,4},{6,5},{7,6},{8,7},{9,8},{10,9},{11,1... | collective-permute-start | bytes 196616 | tf_op jit(solution)/shard_map/ppermute | solution.py:27
  70.5 0.4 fusion.27
  71.5 0.4 fusion.24
  72.6 0.4 fusion.21
  73.5 0.5 collective-permute-done.7
  74.0 1.4 %select_maximum_fusion = bf16[2,64,10,258]{3,1,2,0:T(8,128)(2,1)S(1)} fusion(bf16[2,64,1,256]{3,1,2,0:T(8,128)(2,1)} %collective-permute-done.7, bf16[2,64,8,256]{3,1,2,0:T(8,128)(2,1)S(1)} %get-tuple-element.29, bf16[2,64,1,256]{3,1,2,0:T(8,128)(2,1)S(1)} %collective-permute-done.6), kind=kLoop, calls=%fused_computation.101 | loop fusion | flops 3962880 | bytes 1315840 | tf_op jit(solution)/shard_map/concatenate | solution.py:23
  75.4 0.3 fusion.48
  75.7 1.2 fusion.38
  76.9 0.4 convolution_add_fusion.19
  77.7 0.4 convolution_add_fusion.17
  79.1 0.9 copy-done.7
  80.0 0.8 multiply_reduce_fusion
  80.8 0.4 copy-done.9
  81.2 0.8 convolution_bitcast_fusion.20
  82.3 1.9 %concatenate.51 = f32[74561]{0:T(1024)S(1)} concatenate(f32[1]{0:T(128)} %bitcast.65, f32[73728]{0:T(1024)S(1)} %reshape.147, f32[128]{0:T(128)S(1)} %reshape.148, f32[128]{0:T(128)S(1)} %reshape.149, f32[64]{0:T(128)S(1)} %get-tuple-element.25, f32[512]{0:T(512)S(1)} %reshape.150), dimensions={0} | concatenate | bytes 596488 | tf_op jit(solution)/shard_map/concatenate | solution.py:354
  84.2 46.8 %sum_everywhere.1 = f32[16,40,128]{2,1,0:T(8,128)S(1)} custom-call(f32[16,40,128]{2,1,0:T(8,128)S(1)} %bitcast.430), custom_call_target="tpu_custom_call" | custom-call | tf_op jit(solution)/shard_map/sum_everywhere/pallas_call | solution.py:125
  131.0 0.5 slice.398
  131.5 0.6 slice.402
  132.3 0.6 reshape.156
  133.0 0.6 reshape.155
  133.7 0.7 copy.85
  134.4 1.0 reshape.154
  (104 shorter events, 12.4 us)
Async XLA Ops:
  0.6 0.8 copy-start
  0.7 2.5 %copy-start.20 = (s32[8]{0:T(128)}, s32[8]{0:T(128)S(1)}, u32[]{:S(2)}) copy-start(s32[8]{0:T(128)S(1)} %get-tuple-element.61) | copy-start | bytes 100
  3.2 13.7 %copy-start.6 = (f32[2,64,8,256]{3,1,2,0:T(8,128)}, f32[2,64,8,256]{3,1,2,0:T(8,128)S(1)}, u32[]{:S(2)}) copy-start(f32[2,64,8,256]{3,1,2,0:T(8,128)S(1)} %get-tuple-element.53) | copy-start | bytes 3145732
  3.5 10.9 %copy-start.10 = (bf16[2,9,64,64]{3,2,1,0:T(8,128)(2,1)S(1)}, bf16[2,9,64,64]{3,2,1,0:T(8,128)(2,1)}, u32[]{:S(2)}) copy-start(bf16[2,9,64,64]{3,2,1,0:T(8,128)(2,1)} %param.14) | copy-start | bytes 442372
  3.5 6.7 %collective-permute-start = (bf16[2,64,1,256]{3,1,2,0:T(8,128)(2,1)S(1)}, bf16[2,64,1,256]{3,1,2,0:T(8,128)(2,1)S(1)}, u32[]{:S(2)}, u32[]{:S(2)}) collective-permute-start(bf16[2,64,1,256]{3,1,2,0:T(8,128)(2,1)S(1)} %get-tuple-element.43), channel_id=1, source_target_pairs={{0,1},{1,2},{2,3},{3,4},{4,5},{5,6},{6,7},{7,8},{8,9},{9,10},{10,1... | collective-permute-start | bytes 196616 | tf_op jit(solution)/shard_map/ppermute | solution.py:25
  8.3 5.6 %collective-permute-start.1 = (bf16[2,64,1,256]{3,1,2,0:T(8,128)(2,1)S(1)}, bf16[2,64,1,256]{3,1,2,0:T(8,128)(2,1)S(1)}, u32[]{:S(2)}, u32[]{:S(2)}) collective-permute-start(bf16[2,64,1,256]{3,1,2,0:T(8,128)(2,1)S(1)} %get-tuple-element.44), channel_id=1, source_target_pairs={{1,0},{2,1},{3,2},{4,3},{5,4},{6,5},{7,6},{8,7},{9,8},{10,9},{11,1... | collective-permute-start | bytes 196616 | tf_op jit(solution)/shard_map/ppermute | solution.py:27
  13.9 3.1 %copy-start.13 = (bf16[2,64,1,256]{3,1,2,0:T(8,128)(2,1)}, bf16[2,64,1,256]{3,1,2,0:T(8,128)(2,1)S(1)}, u32[]{:S(2)}) copy-start(bf16[2,64,1,256]{3,1,2,0:T(8,128)(2,1)S(1)} %collective-permute-done.1) | copy-start | bytes 196612
  18.5 11.5 %copy-start.2 = (f32[2,64,8,256]{3,1,2,0:T(8,128)}, f32[2,64,8,256]{3,1,2,0:T(8,128)S(1)}, u32[]{:S(2)}) copy-start(f32[2,64,8,256]{3,1,2,0:T(8,128)S(1)} %get-tuple-element.36) | copy-start | bytes 3145732
  18.5 4.7 %copy-start.17 = (s32[8,256]{1,0:T(8,128)S(1)}, s32[8,256]{1,0:T(8,128)}, u32[]{:S(2)}) copy-start(s32[8,256]{1,0:T(8,128)} %param.12) | copy-start | bytes 24580
  18.8 4.4 %collective-permute-start.2 = (bf16[2,64,1,256]{3,1,2,0:T(8,128)(2,1)S(1)}, bf16[2,64,1,256]{3,1,2,0:T(8,128)(2,1)S(1)}, u32[]{:S(2)}, u32[]{:S(2)}) collective-permute-start(bf16[2,64,1,256]{3,1,2,0:T(8,128)(2,1)S(1)} %get-tuple-element.41), channel_id=1, source_target_pairs={{0,1},{1,2},{2,3},{3,4},{4,5},{5,6},{6,7},{7,8},{8,9},{9,10},{10,1... | collective-permute-start | bytes 196616 | tf_op jit(solution)/shard_map/ppermute | solution.py:25
  20.7 5.6 %collective-permute-start.3 = (bf16[2,64,1,256]{3,1,2,0:T(8,128)(2,1)S(1)}, bf16[2,64,1,256]{3,1,2,0:T(8,128)(2,1)S(1)}, u32[]{:S(2)}, u32[]{:S(2)}) collective-permute-start(bf16[2,64,1,256]{3,1,2,0:T(8,128)(2,1)S(1)} %get-tuple-element.42), channel_id=1, source_target_pairs={{1,0},{2,1},{3,2},{4,3},{5,4},{6,5},{7,6},{8,7},{9,8},{10,9},{11,1... | collective-permute-start | bytes 196616 | tf_op jit(solution)/shard_map/ppermute | solution.py:27
  30.0 0.7 copy-start.16
  30.0 0.7 copy-start.18
  30.7 0.7 copy-start.15
  31.4 8.6 %copy-start.1 = (f32[2,2,8,256]{3,2,1,0:T(8,128)}, f32[2,2,8,256]{3,2,1,0:T(8,128)S(1)}, u32[]{:S(2)}) copy-start(f32[2,2,8,256]{3,2,1,0:T(8,128)S(1)} %get-tuple-element.34.own) | copy-start | bytes 98308
  40.5 1.0 copy-start.4
  42.4 11.5 %collective-permute-start.4 = (bf16[2,64,1,256]{3,1,2,0:T(8,128)(2,1)}, bf16[2,64,1,256]{3,1,2,0:T(8,128)(2,1)}, u32[]{:S(2)}, u32[]{:S(2)}) collective-permute-start(bf16[2,64,1,256]{3,1,2,0:T(8,128)(2,1)} %get-tuple-element.39), channel_id=1, source_target_pairs={{0,1},{1,2},{2,3},{3,4},{4,5},{5,6},{6,7},{7,8},{8,9},{9,10},{10,1... | collective-permute-start | bytes 196616 | tf_op jit(solution)/shard_map/ppermute | solution.py:25
  46.8 7.1 %collective-permute-start.5 = (bf16[2,64,1,256]{3,1,2,0:T(8,128)(2,1)}, bf16[2,64,1,256]{3,1,2,0:T(8,128)(2,1)}, u32[]{:S(2)}, u32[]{:S(2)}) collective-permute-start(bf16[2,64,1,256]{3,1,2,0:T(8,128)(2,1)} %get-tuple-element.40), channel_id=1, source_target_pairs={{1,0},{2,1},{3,2},{4,3},{5,4},{6,5},{7,6},{8,7},{9,8},{10,9},{11,1... | collective-permute-start | bytes 196616 | tf_op jit(solution)/shard_map/ppermute | solution.py:27
  51.5 0.7 copy-start.11
  58.8 1.3 copy-start.3
  60.1 1.2 copy-start.5
  60.1 1.5 %copy-start.8 = (f32[2,64,8,256]{3,1,2,0:T(8,128)S(1)}, f32[2,64,8,256]{3,1,2,0:T(8,128)}, u32[]{:S(2)}) copy-start(f32[2,64,8,256]{3,1,2,0:T(8,128)} %get-tuple-element.54) | copy-start | bytes 3145732
  64.5 9.0 %collective-permute-start.6 = (bf16[2,64,1,256]{3,1,2,0:T(8,128)(2,1)}, bf16[2,64,1,256]{3,1,2,0:T(8,128)(2,1)S(1)}, u32[]{:S(2)}, u32[]{:S(2)}) collective-permute-start(bf16[2,64,1,256]{3,1,2,0:T(8,128)(2,1)} %get-tuple-element.37), channel_id=1, source_target_pairs={{0,1},{1,2},{2,3},{3,4},{4,5},{5,6},{6,7},{7,8},{8,9},{9,10},{10,1... | collective-permute-start | bytes 196616 | tf_op jit(solution)/shard_map/ppermute | solution.py:25
  68.1 5.9 %collective-permute-start.7 = (bf16[2,64,1,256]{3,1,2,0:T(8,128)(2,1)}, bf16[2,64,1,256]{3,1,2,0:T(8,128)(2,1)}, u32[]{:S(2)}, u32[]{:S(2)}) collective-permute-start(bf16[2,64,1,256]{3,1,2,0:T(8,128)(2,1)} %get-tuple-element.38), channel_id=1, source_target_pairs={{1,0},{2,1},{3,2},{4,3},{5,4},{6,5},{7,6},{8,7},{9,8},{10,9},{11,1... | collective-permute-start | bytes 196616 | tf_op jit(solution)/shard_map/ppermute | solution.py:27
  71.5 0.8 copy-start.14
  72.3 1.0 copy-start.12
  78.8 1.2 copy-start.7
  80.0 1.2 copy-start.9
  80.0 1.2 copy-start.19
  80.0 1.2 copy-start.21

commit v2 on v0

v2 whole, which is shorter than its diff:
```python
import jax
import jax.numpy as jnp
from jax import lax
from jax.experimental import pallas as pl
from jax.experimental.pallas import tpu as pltpu
from jax.sharding import PartitionSpec as P

LOSS_SCALE = 16384
MESH_ID = pl.DeviceIdType.MESH
GROUP = 16
MEMS = 8
TILES = 32
HERE = 2
MEMBERS = 16
ROWS = 8
COLS = 256
CH = 64
NOISE = 8
HALO = 4
EXT = ROWS + 2 * HALO
GRID_ROWS = ROWS * TILES
CHUNK = 24
F32 = jnp.float32
BF16 = jnp.bfloat16
eps_norm = 1e-05
smooth_sq = 0.01


def coordinates():
    mem, tile = lax.axis_index("mem"), lax.axis_index("tile")
    return mem // 2, (tile // 2) % 4, (tile // 8) * 2 + mem % 2, tile % 2


def device_at(x, y, z, core):
    return (x * 2 + z % 2, (z // 2) * 8 + y * 2 + core)


def plane_rank():
    x, y, _, _ = coordinates()
    return x * 4 + y


def plane_device(rank):
    _, _, z, core = coordinates()
    return device_at(rank // 4, rank % 4, z, core)


def line_rank():
    _, _, z, core = coordinates()
    return z * 2 + core


def line_device(rank):
    x, y, _, _ = coordinates()
    return device_at(x, y, rank // 2, rank % 2)


def mem_device(rank):
    return (rank, lax.axis_index("tile"))


def others(rank, count):
    return [lax.rem(rank + step, count) for step in range(1, count)]


def modulo(value, base):
    quotient = jnp.floor(value.astype(F32) * (1.0 / base)).astype(jnp.int32)
    rest = value - quotient * base
    rest = jnp.where(rest < 0, rest + base, rest)
    return jnp.where(rest >= base, rest - base, rest)


def noise_row(seed, row):
    channel = lax.broadcasted_iota(jnp.int32, (NOISE, COLS), 0)
    column = lax.broadcasted_iota(jnp.int32, (NOISE, COLS), 1)
    first = modulo(7919 * channel + column + (seed + row * COLS), 65521)
    second = modulo(first * 3001 + 12345, 65521)
    folded = modulo(second, 46337)
    third = modulo(folded * folded + second, 65521)
    fourth = modulo(third * 2897 + 4111, 65521)
    return ((fourth - 32760).astype(F32) / 18914.0).astype(BF16)


def columns_of(shape):
    return lax.broadcasted_iota(jnp.int32, shape, len(shape) - 1)


def from_left(value):
    return jnp.where(columns_of(value.shape) == 0, 0.0, pltpu.roll(value, 1, axis=1))


def from_right(value):
    return jnp.where(columns_of(value.shape) == COLS - 1, 0.0, pltpu.roll(value, COLS - 1, axis=1))


def dot(left, right):
    return jnp.dot(left, right, preferred_element_type=F32)


def dot_rows(left, right):
    return lax.dot_general(left, right, (((1,), (1,)), ((), ())), preferred_element_type=F32)


def diagonal():
    shape = (CH, CH)
    return lax.broadcasted_iota(jnp.int32, shape, 0) == lax.broadcasted_iota(jnp.int32, shape, 1)


def as_column(row):
    return jnp.sum(jnp.where(diagonal(), jnp.broadcast_to(row, (CH, CH)), 0.0), axis=1, keepdims=True)


def as_row(column):
    return jnp.sum(jnp.where(diagonal(), jnp.broadcast_to(column, (CH, CH)), 0.0), axis=0, keepdims=True)


def silu_parts(value):
    gate = 0.5 * jnp.tanh(0.5 * value) + 0.5
    gated = value * gate
    return gated, gate + gated * (1.0 - gate)


def inverse_scale(stream):
    return lax.rsqrt(jnp.sum(stream * stream, axis=0, keepdims=True) * (1.0 / CH) + eps_norm)


def norm_back(grad, normed, inverse):
    mean = jnp.sum(grad * normed, axis=0, keepdims=True) * (1.0 / CH)
    return (grad - normed * mean) * inverse


def step_kernel(
    block_input,
    seeds,
    targets,
    land_mask,
    noise_weight,
    conv_weight,
    block_gain,
    head_weight,
    head_gain,
    predictions,
    grad_conv,
    small_out,
    turned,
    raw,
    noise,
    stream0,
    stream1,
    stream2,
    inverse0,
    inverse1,
    inverse2,
    slope0,
    slope1,
    inputs0,
    inputs1,
    grads0,
    grads1,
    stream_grad,
    head_in,
    forward_taps,
    backward_taps,
    gains,
    edge_out,
    edge_in,
    target_tiles,
    weight_tiles,
    own_pred,
    all_pred,
    pred_grad,
    sums,
    tap_sum,
    parts,
    scattered,
    spread,
    gathered,
    whole,
    small,
    small_in,
    small_line,
    halo_sems,
    mem_sems,
    plane_sems,
    line_sems,
    back_sems,
    small_sems,
    small_line_sems,
):
    mem, tile = lax.axis_index("mem"), lax.axis_index("tile")
    in_plane, in_line = plane_rank(), line_rank()
    below, above = lax.rem(tile + 1, TILES), lax.rem(tile + TILES - 1, TILES)
    plane = [(plane_device(rank), rank) for rank in others(in_plane, GROUP)]
    line = [(line_device(rank), rank) for rank in others(in_line, GROUP)]
    members = [(mem_device(rank), rank) for rank in others(mem, MEMS)]

    barrier = pltpu.get_barrier_semaphore()
    for device in [(mem, below), (mem, above)] + [d for d, _ in plane + line + members]:
        pl.semaphore_signal(barrier, inc=1, device_id=device, device_id_type=MESH_ID)

    def send(source, target, sems, slot, device):
        copy = pltpu.make_async_remote_copy(
            src_ref=source,
            dst_ref=target,
            send_sem=sems.at[0, slot],
            recv_sem=sems.at[1, slot],
            device_id=device,
            device_id_type=MESH_ID,
        )
        copy.start()
        return copy

    def wait(copies):
        for copy in copies:
            copy.wait()

    for m in range(HERE):
        for half in range(2):
            lanes = pl.ds(128 * half, 128)
            turned[m, half] = block_input[m, :, :, lanes].astype(F32).reshape(CH * ROWS, 128)
            for r in range(ROWS):
                raw[HALO + r, m, :, lanes] = turned[m, half, pl.ds(r, CH, stride=ROWS), :].astype(BF16)
    for side, start in ((0, 0), (1, ROWS - 2)):
        edge_out[side] = jnp.zeros((8, COLS), F32)
        for v in range(2):
            edge_out[side, pl.ds(2 * v, 2), :] = targets[v, pl.ds(start, 2), :]
        edge_out[side, pl.ds(4, 2), :] = land_mask[pl.ds(start, 2), :].astype(F32)

    pl.semaphore_wait(barrier, 2 + 2 * (GROUP - 1) + (MEMS - 1))

    halo_copies = [
        send(raw.at[pl.ds(HALO, HALO)], raw.at[pl.ds(HALO + ROWS, HALO)], halo_sems, 0, (mem, above)),
        send(raw.at[pl.ds(ROWS, HALO)], raw.at[pl.ds(0, HALO)], halo_sems, 1, (mem, below)),
        send(edge_out.at[0], edge_in.at[1], halo_sems, 2, (mem, above)),
        send(edge_out.at[1], edge_in.at[0], halo_sems, 3, (mem, below)),
    ]

    unit = diagonal().astype(F32).astype(BF16)
    blank = jnp.zeros((CH, CH), BF16)
    for b in range(2):
        for dc in range(3):
            taps = [conv_weight[b, 3 * dr + dc] for dr in range(3)]
            turned_taps = [dot_rows(unit, tap).astype(BF16) for tap in taps]
            for ro in range(2):
                at = pl.ds((2 * dc + ro) * CH, CH)
                ahead = [blank] * ro + turned_taps + [blank] * (1 - ro)
                forward_taps[b, at, :] = dot_rows(unit, jnp.concatenate(ahead, axis=0)).astype(BF16)
                back = [blank] * ro + taps[::-1] + [blank] * (1 - ro)
                backward_taps[b, at, :] = dot_rows(unit, jnp.concatenate(back, axis=0)).astype(BF16)
    columns = [block_gain[pl.ds(0, 1), :], block_gain[pl.ds(1, 1), :], head_gain[...]]
    columns += [head_weight[pl.ds(v, 1), :].astype(F32) for v in range(2)]
    for at, row in enumerate(columns):
        gains[at] = jnp.broadcast_to(as_column(row), (CH, COLS))
    for at in range(5):
        sums[at] = jnp.zeros((CH, COLS), F32)
    sums_noise = [jnp.zeros((CH, NOISE), F32)]

    def inside(e):
        row = tile * ROWS - HALO + e
        return jnp.where((row >= 0) & (row < GRID_ROWS), 1.0, 0.0).astype(F32)

    def entry(e):
        row = jnp.clip(tile * ROWS - HALO + e, 0, GRID_ROWS - 1)
        for m in range(HERE):
            field = noise_row(seeds[m], row)
            noise[e, m] = field.astype(F32)
            stream = raw[e, m].astype(F32) + dot(noise_weight[...], field)
            stream0[e, m] = stream
            inverse = inverse_scale(stream)
            inverse0[e, m] = jnp.broadcast_to(inverse, (8, COLS))
            inputs0[e, m] = (stream * (inverse * inside(e)) * gains[0]).astype(BF16)

    def forward(b, e):
        source, stream_in, stream_out, slope = (
            (inputs0, stream0, stream1, slope0),
            (inputs1, stream1, stream2, slope1),
        )[b]
        for m in range(HERE):
            window = source[pl.ds(e - 1, 4), m].reshape(4 * CH, COLS)
            taken = dot(forward_taps[b], window)
            for ro in range(2):
                left, middle, right = [taken[(2 * dc + ro) * CH : (2 * dc + ro + 1) * CH] for dc in range(3)]
                gated, bent = silu_parts(middle + from_left(left) + from_right(right))
                slope[e + ro, m] = bent
                stream = stream_in[e + ro, m] + gated
                stream_out[e + ro, m] = stream
                inverse = inverse_scale(stream)
                if b == 0:
                    inverse1[e + ro, m] = jnp.broadcast_to(inverse, (8, COLS))
                    inputs1[e + ro, m] = (stream * (inverse * inside(e + ro)) * gains[1]).astype(BF16)
                else:
                    inverse2[e + ro, m] = jnp.broadcast_to(inverse, (8, COLS))
                    headed = (stream * inverse * gains[2]).astype(BF16)
                    head_in[e + ro, m] = headed
                    found = dot(head_weight[...], headed)
                    place(own_pred, m, e + ro, found)

    def spots(e):
        if isinstance(e, int) and not HALO <= e < HALO + ROWS:
            at = (e - 2) if e < HALO else (e - HALO - ROWS + 2)
            return [(2, at), (2, at + 4)]
        return [(0, e - HALO), (1, e - HALO)]

    def place(ref, m, e, pair):
        for v, (part, at) in enumerate(spots(e)):
            ref[m, part, pl.ds(at, 1), :] = pair[v : v + 1]

    def over(first, count, body):
        lax.fori_loop(0, count, lambda i, c: (body(first + 2 * i), c)[1], 0)

    def over_rows(first, count, body):
        lax.fori_loop(0, count, lambda i, c: (body(first + i), c)[1], 0)

    over_rows(HALO, ROWS, entry)
    over(5, 3, lambda e: forward(0, e))
    wait(halo_copies)
    over_rows(0, HALO, entry)
    over_rows(HALO + ROWS, HALO, entry)
    over(1, 2, lambda e: forward(0, e))
    over(11, 2, lambda e: forward(0, e))
    forward(1, 2)
    forward(1, 12)
    over(4, 4, lambda e: forward(1, e))

    all_pred[mem] = own_pred[...]
    pred_copies = [
        send(own_pred, all_pred.at[mem], mem_sems, step, device) for step, (device, _) in enumerate(members)
    ]
    predictions[...] = own_pred[:, pl.ds(0, 2)]
    for v in range(2):
        target_tiles[v] = targets[v]
        for side in range(2):
            target_tiles[2, pl.ds(4 * v + 2 * side, 2), :] = edge_in[side, pl.ds(2 * v, 2), :]
            weight_tiles[1, pl.ds(4 * v + 2 * side, 2), :] = edge_in[side, pl.ds(4, 2), :]
    weight_tiles[0] = land_mask[...].astype(F32)
    own_row = lax.broadcasted_iota(jnp.int32, (8, COLS), 0)
    side_row = own_row % 4
    side_row = jnp.where(side_row < 2, side_row - 2, side_row + ROWS - 2)
    for at, rows in enumerate((own_row, side_row)):
        area = 1.0 - 2.0 * (rows + tile * ROWS).astype(F32) / (3.0 * GRID_ROWS)
        weight_tiles[at] = area * (1.0 + weight_tiles[at])
    wait(pred_copies)

    def lengths(own, edge):
        squares = edge * edge
        return own[0] * own[0] + own[1] * own[1] + smooth_sq, squares + pltpu.roll(squares, 4, axis=0) + smooth_sq

    cells = GRID_ROWS * COLS
    loss_tile = jnp.zeros((8, COLS), F32)
    for m in range(HERE):
        mine = [own_pred[m, part] for part in range(3)]

        def pull_from(n, carry):
            pulls, total = carry
            gaps = [mine[part] - all_pred[n // HERE, lax.rem(n, HERE), part] for part in range(3)]
            own_sq, edge_sq = lengths(gaps[:2], gaps[2])
            own_inv, edge_inv = lax.rsqrt(own_sq), lax.rsqrt(edge_sq)
            pulls = tuple(
                pull + gap * inv for pull, gap, inv in zip(pulls, gaps, (own_inv, own_inv, edge_inv))
            )
            return pulls, total + own_sq * own_inv

        blank_tile = jnp.zeros((8, COLS), F32)
        pulls, total = lax.fori_loop(0, MEMBERS, pull_from, ((blank_tile,) * 3, blank_tile - smooth_sq**0.5))
        misses = [mine[part] - target_tiles[part] for part in range(3)]
        own_sq, edge_sq = lengths(misses[:2], misses[2])
        own_inv, edge_inv = lax.rsqrt(own_sq), lax.rsqrt(edge_sq)
        loss_tile += weight_tiles[0] * (
            own_sq * own_inv * (1.0 / MEMBERS) - total * (1.0 / (2.0 * MEMBERS * (MEMBERS - 1)))
        )
        for part, inv in enumerate((own_inv, own_inv, edge_inv)):
            factor = weight_tiles[part // 2] * (LOSS_SCALE / cells)
            grad = factor * (
                misses[part] * inv * (1.0 / MEMBERS) - pulls[part] * (1.0 / (MEMBERS * (MEMBERS - 1.0)))
            )
            pred_grad[m, part] = grad.astype(BF16).astype(F32)

    def top(e, own):
        for m in range(HERE):
            (part0, at0), (part1, at1) = spots(e)
            pull0 = pred_grad[m, part0, pl.ds(at0, 1), :]
            pull1 = pred_grad[m, part1, pl.ds(at1, 1), :]
            grad = gains[3] * pull0 + gains[4] * pull1
            inverse = inverse2[e, m, pl.ds(0, 1), :]
            normed = stream2[e, m] * inverse
            if own:
                headed = head_in[e, m].astype(F32)
                sums[2] += grad * normed
                sums[3] += headed * pull0
                sums[4] += headed * pull1
            grad = norm_back(grad * gains[2], normed, inverse)
            stream_grad[e, m] = grad
            grads1[e, m] = (grad * (slope1[e, m] * inside(e))).astype(BF16)

    def tap_grads(grads, inputs):
        tap_sum[...] = jnp.zeros_like(tap_sum)

        def one(e):
            for m in range(HERE):
                grad = grads[e, m].astype(F32)
                shifts = [from_right(grad), grad, from_left(grad)]
                shifts = jnp.concatenate([shift.astype(BF16) for shift in shifts], axis=0)
                window = inputs[pl.ds(e - 1, 3), m].reshape(3 * CH, COLS)
                tap_sum[:, pl.ds(0, 3 * CH)] += dot_rows(shifts, window)

        over_rows(HALO, ROWS, one)

    def backward(b, e, last):
        source, stream, inverses = ((grads0, stream0, inverse0), (grads1, stream1, inverse1))[b]
        for m in range(HERE):
            window = source[pl.ds(e - 1, 4), m].reshape(4 * CH, COLS)
            taken = dot(backward_taps[b], window)
            for ro in range(2):
                left, middle, right = [taken[(2 * dc + ro) * CH : (2 * dc + ro + 1) * CH] for dc in range(3)]
                grad = middle + from_right(left) + from_left(right)
                inverse = inverses[e + ro, m, pl.ds(0, 1), :]
                normed = stream[e + ro, m] * inverse
                counted = jnp.where((e + ro >= HALO) & (e + ro < HALO + ROWS), 1.0, 0.0).astype(F32)
                sums[b] += grad * (normed * counted)
                total = stream_grad[e + ro, m] + norm_back(grad * gains[b], normed, inverse)
                if b == 1:
                    stream_grad[e + ro, m] = total
                    grads0[e + ro, m] = (total * (slope0[e + ro, m] * inside(e + ro))).astype(BF16)
                else:
                    last(e + ro, m, total.astype(BF16))

    def to_parts(b):
        for at in range(GROUP):
            parts[b, at] = tap_sum[pl.ds(CHUNK * (at // 2), CHUNK), pl.ds(128 * (at % 2), 128)]

    def scatter(b):
        return [
            send(parts.at[b, rank], scattered.at[b, step], plane_sems.at[b], step, device)
            for step, (device, rank) in enumerate(plane)
        ]

    def spread_out(b):
        total = parts[b, in_plane]
        for step in range(GROUP - 1):
            total = total + scattered[b, step]
        spread[b, in_line] = total
        return [
            send(spread.at[b, in_line], spread.at[b, in_line], line_sems.at[b], step, device)
            for step, (device, _) in enumerate(line)
        ]

    def gather(b):
        total = spread[b, 0]
        for rank in range(1, GROUP):
            total = total + spread[b, rank]
        gathered[b, in_plane] = total
        return [
            send(gathered.at[b, in_plane], gathered.at[b, in_plane], back_sems.at[b], step, device)
            for step, (device, _) in enumerate(plane)
        ]

    def finish(b):
        for at in range(GROUP):
            whole[pl.ds(CHUNK * (at // 2), CHUNK), pl.ds(128 * (at % 2), 128)] = gathered[b, at]
        for dr in range(3):
            for dc in range(3):
                grad_conv[b, 3 * dr + dc] = whole[pl.ds(CH * dc, CH), pl.ds(CH * dr, CH)]

    for e in (2, 3, 12, 13):
        top(e, False)
    over_rows(HALO, ROWS, lambda e: top(e, True))
    tap_grads(grads1, inputs1)
    to_parts(1)
    plane_1 = scatter(1)
    over(3, 5, lambda e: backward(1, e, None))
    tap_grads(grads0, inputs0)
    to_parts(0)
    plane_0 = scatter(0)
    wait(plane_1)
    line_1 = spread_out(1)

    small[...] = jnp.zeros_like(small)
    sum_noise = tap_sum.at[pl.ds(0, CH), pl.ds(0, NOISE)]
    sum_noise[...] = jnp.zeros((CH, NOISE), F32)

    def last(e, m, entry_grad):
        sum_noise[...] += dot_rows(entry_grad, noise[e, m].astype(BF16))

    over(4, 4, lambda e: backward(0, e, last))
    column = lax.broadcasted_iota(jnp.int32, (CH, NOISE), 1)
    late = sum_noise[...]
    for at in range(5):
        small[pl.ds(at, 1), pl.ds(0, CH)] = as_row(jnp.sum(sums[at], axis=1, keepdims=True))
    for k in range(NOISE):
        picked = jnp.sum(jnp.where(column == k, late, 0.0), axis=1, keepdims=True)
        small[pl.ds(5 + k, 1), pl.ds(0, CH)] = as_row(picked)
    loss = jnp.sum(jnp.sum(loss_tile, axis=0, keepdims=True), axis=1, keepdims=True) * (1.0 / cells)
    small[pl.ds(13, 1), :] = jnp.broadcast_to(loss, (1, 128))
    small_in[in_plane] = small[...]
    small_1 = [
        send(small, small_in.at[in_plane], small_sems, step, device) for step, (device, _) in enumerate(plane)
    ]
    wait(plane_0)
    line_0 = spread_out(0)
    wait(line_1)
    back_1 = gather(1)
    wait(small_1)
    total = small_in[0]
    for rank in range(1, GROUP):
        total = total + small_in[rank]
    small_line[in_line] = total
    small_2 = [
        send(small_line.at[in_line], small_line.at[in_line], small_line_sems, step, device)
        for step, (device, _) in enumerate(line)
    ]
    wait(line_0)
    back_0 = gather(0)
    wait(back_1)
    finish(1)
    wait(small_2)
    total = small_line[0]
    for rank in range(1, GROUP):
        total = total + small_line[rank]
    small_out[...] = total
    wait(back_0)
    finish(0)


def on_device(
    block_input,
    member_seeds,
    targets,
    land_mask,
    noise_weight,
    conv_weight,
    block_gain,
    head_weight,
    head_gain,
):
    vmem = pl.BlockSpec(memory_space=pltpu.VMEM)
    smem = pl.BlockSpec(memory_space=pltpu.SMEM)

    def field(*shape):
        return pltpu.VMEM((EXT, HERE) + shape, F32)

    def half(*shape):
        return pltpu.VMEM((EXT, HERE) + shape, BF16)

    def sems(*shape):
        return pltpu.SemaphoreType.DMA(shape)

    scratch = dict(
        turned=pltpu.VMEM((HERE, 2, CH * ROWS, 128), F32),
        raw=half(CH, COLS),
        noise=field(NOISE, COLS),
        stream0=field(CH, COLS),
        stream1=field(CH, COLS),
        stream2=field(CH, COLS),
        inverse0=field(8, COLS),
        inverse1=field(8, COLS),
        inverse2=field(8, COLS),
        slope0=field(CH, COLS),
        slope1=field(CH, COLS),
        inputs0=half(CH, COLS),
        inputs1=half(CH, COLS),
        grads0=half(CH, COLS),
        grads1=half(CH, COLS),
        stream_grad=field(CH, COLS),
        head_in=half(CH, COLS),
        forward_taps=pltpu.VMEM((2, 6 * CH, 4 * CH), BF16),
        backward_taps=pltpu.VMEM((2, 6 * CH, 4 * CH), BF16),
        gains=pltpu.VMEM((5, CH, COLS), F32),
        edge_out=pltpu.VMEM((2, 8, COLS), F32),
        edge_in=pltpu.VMEM((2, 8, COLS), F32),
        target_tiles=pltpu.VMEM((3, 8, COLS), F32),
        weight_tiles=pltpu.VMEM((2, 8, COLS), F32),
        own_pred=pltpu.VMEM((HERE, 3, 8, COLS), F32),
        all_pred=pltpu.VMEM((MEMS, HERE, 3, 8, COLS), F32),
        pred_grad=pltpu.VMEM((HERE, 3, 8, COLS), F32),
        sums=pltpu.VMEM((5, CH, COLS), F32),
        tap_sum=pltpu.VMEM((3 * CH, 256), F32),
        parts=pltpu.VMEM((2, GROUP, CHUNK, 128), F32),
        scattered=pltpu.VMEM((2, GROUP - 1, CHUNK, 128), F32),
        spread=pltpu.VMEM((2, GROUP, CHUNK, 128), F32),
        gathered=pltpu.VMEM((2, GROUP, CHUNK, 128), F32),
        whole=pltpu.VMEM((3 * CH, 256), F32),
        small=pltpu.VMEM((16, 128), F32),
        small_in=pltpu.VMEM((GROUP, 16, 128), F32),
        small_line=pltpu.VMEM((GROUP, 16, 128), F32),
        halo_sems=sems(2, 4),
        mem_sems=sems(2, MEMS - 1),
        plane_sems=sems(2, 2, GROUP - 1),
        line_sems=sems(2, 2, GROUP - 1),
        back_sems=sems(2, 2, GROUP - 1),
        small_sems=sems(2, GROUP - 1),
        small_line_sems=sems(2, GROUP - 1),
    )
    predictions, grad_conv, small = pl.pallas_call(
        step_kernel,
        out_shape=(
            jax.ShapeDtypeStruct((HERE, 2, ROWS, COLS), F32),
            jax.ShapeDtypeStruct((2, 9, CH, CH), F32),
            jax.ShapeDtypeStruct((16, 128), F32),
        ),
        in_specs=[vmem, smem] + [vmem] * 7,
        out_specs=(vmem, vmem, vmem),
        scratch_shapes=list(scratch.values()),
        compiler_params=pltpu.CompilerParams(
            collective_id=0, has_side_effects=True, vmem_limit_bytes=48 * 2**20
        ),
        name="train_step",
    )(
        block_input,
        member_seeds,
        targets,
        land_mask,
        noise_weight,
        conv_weight,
        block_gain,
        head_weight,
        head_gain.reshape(1, CH),
    )
    return (
        small[13, 0],
        predictions,
        grad_conv,
        small[0:2, :CH],
        small[3:5, :CH],
        small[2, :CH],
        small[5:13, :CH].T,
    )


def solution(mesh):
    return jax.shard_map(
        on_device,
        mesh=mesh,
        in_specs=(
            P("mem", None, "tile", None),
            P("mem"),
            P(None, "tile", None),
            P("tile", None),
            P(),
            P(),
            P(),
            P(),
            P(),
        ),
        out_specs=(P(), P("mem", None, "tile", None), P(), P(), P(), P(), P()),
        check_vma=False,
    )
```

time: 495 us -> 73.3 us (0.15)
  waiting for transfers between devices: 292 us -> 0 us
  blocking collectives: 113 us -> 0 us
  Pallas kernels: 0 us -> 65.2 us
  matrix products: 28 us -> 0 us
  starting transfers between devices: 26.3 us -> 0 us
  between operations: 16.2 us -> 0.73 us
  other arithmetic: 8.17 us -> 0 us
    psum x2 -> x0, waiting for transfers between devices: 285 us -> none  [the longest x1 285 us: on_device(): lax.psum((partials[0], partials[1], partials[2], partials[3], partials[4]...]
    psum x2 -> x0, blocking collectives: 90.3 us -> none  [the longest x1 73.7 us: on_device(): lax.psum((partials[0], partials[1], partials[2], partials[3], partials[4]...]
    pallas_call x0 -> x1, Pallas kernels: none -> 65.2 us  [on_device(): pl.pallas_call(step_kernel, out_shape=(jax.ShapeDtypeStruct((HERE, 2, ROW...]
    dot_general x59 -> x0, matrix products: 28 us -> none  [the longest x18 10.1 us: conv_rows(): jnp.einsum('oi,morw->mirw', weights[3 * offset_r + offset_c], window, pre...]
    ppermute x8 -> x0, starting transfers between devices: 26.3 us -> none  [the longest x4 17.9 us: extended(): lax.ppermute(tail, axis, [(i, (i + 1) % count) for i in range(ends)])]
    all_gather x1 -> x0, blocking collectives: 23.2 us -> none  [on_device(): lax.all_gather(predictions, 'mem', axis=0, tiled=True)[None]]
    ppermute x8 -> x0, waiting for transfers between devices: 6.71 us -> none  [the longest x4 6.7 us: extended(): lax.ppermute(head, axis, [((i + 1) % count, i) for i in range(ends)])]
  transfers between devices with their start and end apart: 10 -> 0, of which waited for: 3 -> 0; matrix products, arithmetic and copies ran while one was open for 3% -> 0% of each run, Pallas kernels for 0% -> 0%
where the time goes in v2:
time: 73.3 us; the launch traced here: 73.1 us
  Pallas kernels  65.2 us (89%)
  local copies, waits for them, and re-layouts  7.14 us (10%)
    pallas_call x1, Pallas kernels, on_device(): pl.pallas_call(step_kernel, out_shape=(jax.ShapeDtypeStruct((HERE, 2, ROW...  65.2 us
    unnamed x19, local copies, waits for them, and re-layouts  4.95 us

profile of v2, /device:TPU:1, one launch (start us, length us, event | category | flops | bytes accessed | tf_op | source)
XLA Modules:
  0.0 73.1 jit_solution(2764391056037558044)
XLA Ops:
  0.6 0.0 copy-start.2
  0.6 0.0 copy-start.4
  0.7 0.0 copy-start.5
  0.7 0.0 copy-start.6
  0.7 0.0 copy-start.7
  0.7 0.8 %copy.16.noise_weight = bf16[64,8]{1,0:T(8,128)(2,1)S(1)} copy(bf16[64,8]{0,1:T(8,128)(2,1)} %param.13) | data formatting | bytes 2048 | tf_op args[4]
  1.5 0.0 copy-done.2
  1.5 0.0 copy-done.4
  1.5 0.0 copy-done.5
  1.5 0.0 copy-done.6
  1.5 0.0 copy-done.7
  1.5 0.0 copy-start
  1.5 1.0 %copy-done = bf16[2,64,8,256]{3,2,1,0:T(8,128)(2,1)S(1)} copy-done((bf16[2,64,8,256]{3,2,1,0:T(8,128)(2,1)S(1)}, bf16[2,64,8,256]{3,2,1,0:T(8,128)(2,1)}, u32[]{:S(2)}) %copy-start) | copy-done | bytes 524312
  2.6 0.0 copy-start.1
  2.6 1.0 %copy-done.1 = bf16[2,9,64,64]{3,2,1,0:T(8,128)(2,1)S(1)} copy-done((bf16[2,9,64,64]{3,2,1,0:T(8,128)(2,1)S(1)}, bf16[2,9,64,64]{3,2,1,0:T(8,128)(2,1)}, u32[]{:S(2)}) %copy-start.1) | copy-done | bytes 147480
  3.5 0.0 copy-start.3
  3.5 0.7 copy-done.3
  4.2 65.2 %train_step.1 = (f32[2,2,8,256]{3,2,1,0:T(8,128)S(1)}, f32[2,9,64,64]{3,2,1,0:T(8,128)S(1)}, f32[16,128]{1,0:T(8,128)S(1)}) custom-call(bf16[2,64,8,256]{3,2,1,0:T(8,128)(2,1)S(1)} %copy-done, s32[2]{0:T(128)S(1)} %copy-done.5, f32[2,8,256]{2,1,0:T(8,128)S(1)} %copy-done.2, s32[8,256]{1,0:T(8,128)S(1)} %copy-done.3, bf16[64,8]{1,0:T(8,128)(2,1)S(1)} %copy.16.noise_weight, ...), custom_call_target="tpu_custom_call" | custom-call | tf_op jit(solution)/shard_map/train_step/pallas_call | solution.py:593
  69.5 0.5 slice.15
  70.0 0.5 slice_bitcast_fusion.1
  70.5 0.6 fusion
  71.1 0.6 slice_bitcast_fusion
  71.7 0.6 copy.19
  72.3 0.8 %copy.20 = f32[2,9,64,64]{3,2,1,0:T(8,128)} copy(f32[2,9,64,64]{3,2,1,0:T(8,128)S(1)} %get-tuple-element.24) | data formatting | bytes 589824
Async XLA Ops:
  0.6 0.9 %copy-start.2 = (f32[2,8,256]{2,1,0:T(8,128)S(1)}, f32[2,8,256]{2,1,0:T(8,128)}, u32[]{:S(2)}) copy-start(f32[2,8,256]{2,1,0:T(8,128)} %targets.1) | copy-start | bytes 49156
  0.6 0.8 %copy-start.4 = (f32[2,64]{1,0:T(2,128)S(1)}, f32[2,64]{1,0:T(2,128)}, u32[]{:S(2)}) copy-start(f32[2,64]{1,0:T(2,128)} %block_gain.1) | copy-start | bytes 1540
  0.7 0.8 %copy-start.5 = (s32[2]{0:T(128)S(1)}, s32[2]{0:T(128)}, u32[]{:S(2)}) copy-start(s32[2]{0:T(128)} %seeds.1) | copy-start | bytes 28
  0.7 0.8 %copy-start.6 = (bf16[2,64]{1,0:T(2,128)(2,1)S(1)}, bf16[2,64]{1,0:T(2,128)(2,1)}, u32[]{:S(2)}) copy-start(bf16[2,64]{1,0:T(2,128)(2,1)} %head_weight.1) | copy-start | bytes 772
  0.7 0.8 %copy-start.7 = (f32[64]{0:T(128)S(1)}, f32[64]{0:T(128)}, u32[]{:S(2)}) copy-start(f32[64]{0:T(128)} %param.17) | copy-start | bytes 772
  1.5 1.0 %copy-start = (bf16[2,64,8,256]{3,2,1,0:T(8,128)(2,1)S(1)}, bf16[2,64,8,256]{3,2,1,0:T(8,128)(2,1)}, u32[]{:S(2)}) copy-start(bf16[2,64,8,256]{3,2,1,0:T(8,128)(2,1)} %block_input.1) | copy-start | bytes 1572868
  2.6 1.0 %copy-start.1 = (bf16[2,9,64,64]{3,2,1,0:T(8,128)(2,1)S(1)}, bf16[2,9,64,64]{3,2,1,0:T(8,128)(2,1)}, u32[]{:S(2)}) copy-start(bf16[2,9,64,64]{3,2,1,0:T(8,128)(2,1)} %conv_weight.1) | copy-start | bytes 442372
  3.5 0.7 copy-start.3

commit v3 on v2

--- a/solution.py
+++ b/solution.py
@@ -20,6 +20,7 @@
 EXT = ROWS + 2 * HALO
 GRID_ROWS = ROWS * TILES
 CHUNK = 24
+VMEM_BYTES = 63 * 2**20
 F32 = jnp.float32
 BF16 = jnp.bfloat16
 eps_norm = 1e-05
@@ -86,11 +87,13 @@
 
 
 def from_left(value):
-    return jnp.where(columns_of(value.shape) == 0, 0.0, pltpu.roll(value, 1, axis=1))
+    return jnp.where(columns_of(value.shape) == 0, jnp.zeros((), value.dtype), pltpu.roll(value, 1, axis=1))
 
 
 def from_right(value):
-    return jnp.where(columns_of(value.shape) == COLS - 1, 0.0, pltpu.roll(value, COLS - 1, axis=1))
+    return jnp.where(
+        columns_of(value.shape) == COLS - 1, jnp.zeros((), value.dtype), pltpu.roll(value, COLS - 1, axis=1)
+    )
 
 
 def dot(left, right):
@@ -130,6 +133,18 @@
 
 
 def step_kernel(
+    block_input_far,
+    seeds_far,
+    targets_far,
+    land_mask_far,
+    noise_weight_far,
+    conv_weight_far,
+    block_gain_far,
+    head_weight_far,
+    head_gain_far,
+    predictions,
+    gathered,
+    small_out,
     block_input,
     seeds,
     targets,
@@ -139,9 +154,7 @@
     block_gain,
     head_weight,
     head_gain,
-    predictions,
-    grad_conv,
-    small_out,
+    load_sems,
     turned,
     raw,
     noise,
@@ -161,6 +174,7 @@
     head_in,
     forward_taps,
     backward_taps,
+    noise_taps,
     gains,
     edge_out,
     edge_in,
@@ -174,8 +188,6 @@
     parts,
     scattered,
     spread,
-    gathered,
-    whole,
     small,
     small_in,
     small_line,
@@ -192,7 +204,27 @@
     below, above = lax.rem(tile + 1, TILES), lax.rem(tile + TILES - 1, TILES)
     plane = [(plane_device(rank), rank) for rank in others(in_plane, GROUP)]
     line = [(line_device(rank), rank) for rank in others(in_line, GROUP)]
+    groups, ranks = ((plane, line), (line, plane)), ((in_plane, in_line), (in_line, in_plane))
     members = [(mem_device(rank), rank) for rank in others(mem, MEMS)]
+
+    loads = [
+        pltpu.make_async_copy(far, near, load_sems.at[at])
+        for at, (far, near) in enumerate(
+            (
+                (block_input_far, block_input),
+                (seeds_far, seeds),
+                (targets_far, targets),
+                (land_mask_far, land_mask),
+                (noise_weight_far, noise_weight),
+                (conv_weight_far, conv_weight),
+                (block_gain_far, block_gain),
+                (head_weight_far, head_weight),
+                (head_gain_far, head_gain),
+            )
+        )
+    ]
+    for load in loads:
+        load.start()
 
     barrier = pltpu.get_barrier_semaphore()
     for device in [(mem, below), (mem, above)] + [d for d, _ in plane + line + members]:
@@ -214,6 +246,7 @@
         for copy in copies:
             copy.wait()
 
+    wait(loads)
     for m in range(HERE):
         for half in range(2):
             lanes = pl.ds(128 * half, 128)
@@ -228,12 +261,18 @@
 
     pl.semaphore_wait(barrier, 2 + 2 * (GROUP - 1) + (MEMS - 1))
 
-    halo_copies = [
-        send(raw.at[pl.ds(HALO, HALO)], raw.at[pl.ds(HALO + ROWS, HALO)], halo_sems, 0, (mem, above)),
-        send(raw.at[pl.ds(ROWS, HALO)], raw.at[pl.ds(0, HALO)], halo_sems, 1, (mem, below)),
-        send(edge_out.at[0], edge_in.at[1], halo_sems, 2, (mem, above)),
-        send(edge_out.at[1], edge_in.at[0], halo_sems, 3, (mem, below)),
+    def halo(up, down, up_to, down_to, slot):
+        return [
+            send(raw.at[pl.ds(up, 2)], raw.at[pl.ds(up_to, 2)], halo_sems, slot, (mem, above)),
+            send(raw.at[pl.ds(down, 2)], raw.at[pl.ds(down_to, 2)], halo_sems, slot + 1, (mem, below)),
+        ]
+
+    near_copies = halo(4, 10, 12, 2, 0)
+    near_copies += [
+        send(edge_out.at[0], edge_in.at[1], halo_sems, 4, (mem, above)),
+        send(edge_out.at[1], edge_in.at[0], halo_sems, 5, (mem, below)),
     ]
+    far_copies = halo(6, 8, 14, 0, 2)
 
     unit = diagonal().astype(F32).astype(BF16)
     blank = jnp.zeros((CH, CH), BF16)
@@ -247,35 +286,38 @@
                 forward_taps[b, at, :] = dot_rows(unit, jnp.concatenate(ahead, axis=0)).astype(BF16)
                 back = [blank] * ro + taps[::-1] + [blank] * (1 - ro)
                 backward_taps[b, at, :] = dot_rows(unit, jnp.concatenate(back, axis=0)).astype(BF16)
+    noise_taps[...] = dot_rows(unit, noise_weight[...]).astype(BF16)
     columns = [block_gain[pl.ds(0, 1), :], block_gain[pl.ds(1, 1), :], head_gain[...]]
     columns += [head_weight[pl.ds(v, 1), :].astype(F32) for v in range(2)]
     for at, row in enumerate(columns):
         gains[at] = jnp.broadcast_to(as_column(row), (CH, COLS))
     for at in range(5):
         sums[at] = jnp.zeros((CH, COLS), F32)
-    sums_noise = [jnp.zeros((CH, NOISE), F32)]
+    tap_sum[...] = jnp.zeros_like(tap_sum)
 
     def inside(e):
         row = tile * ROWS - HALO + e
         return jnp.where((row >= 0) & (row < GRID_ROWS), 1.0, 0.0).astype(F32)
 
-    def entry(e):
+    def make_noise(e):
         row = jnp.clip(tile * ROWS - HALO + e, 0, GRID_ROWS - 1)
         for m in range(HERE):
-            field = noise_row(seeds[m], row)
-            noise[e, m] = field.astype(F32)
-            stream = raw[e, m].astype(F32) + dot(noise_weight[...], field)
+            noise[e, m] = noise_row(seeds[m], row).astype(F32)
+
+    def entry(e):
+        for m in range(HERE):
+            stream = raw[e, m].astype(F32) + dot(noise_taps[...], noise[e, m].astype(BF16))
             stream0[e, m] = stream
             inverse = inverse_scale(stream)
             inverse0[e, m] = jnp.broadcast_to(inverse, (8, COLS))
             inputs0[e, m] = (stream * (inverse * inside(e)) * gains[0]).astype(BF16)
 
-    def forward(b, e):
+    def forward(b, e, ms=range(HERE)):
         source, stream_in, stream_out, slope = (
             (inputs0, stream0, stream1, slope0),
             (inputs1, stream1, stream2, slope1),
         )[b]
-        for m in range(HERE):
+        for m in ms:
             window = source[pl.ds(e - 1, 4), m].reshape(4 * CH, COLS)
             taken = dot(forward_taps[b], window)
             for ro in range(2):
@@ -303,83 +345,94 @@
 
     def place(ref, m, e, pair):
         for v, (part, at) in enumerate(spots(e)):
-            ref[m, part, pl.ds(at, 1), :] = pair[v : v + 1]
+            ref[part, m, pl.ds(at, 1), :] = pair[v : v + 1]
 
     def over(first, count, body):
-        lax.fori_loop(0, count, lambda i, c: (body(first + 2 * i), c)[1], 0)
+        for i in range(count):
+            body(first + 2 * i)
 
     def over_rows(first, count, body):
-        lax.fori_loop(0, count, lambda i, c: (body(first + i), c)[1], 0)
-
+        for i in range(count):
+            body(first + i)
+
+    def share(first, count, sems):
+        parts_here = pl.ds(first, count)
+        all_pred[mem, parts_here] = own_pred[parts_here]
+        return [
+            send(own_pred.at[parts_here], all_pred.at[mem, parts_here], sems, step, device)
+            for step, (device, _) in enumerate(members)
+        ]
+
+    over_rows(HALO, ROWS, make_noise)
     over_rows(HALO, ROWS, entry)
     over(5, 3, lambda e: forward(0, e))
-    wait(halo_copies)
-    over_rows(0, HALO, entry)
-    over_rows(HALO + ROWS, HALO, entry)
-    over(1, 2, lambda e: forward(0, e))
-    over(11, 2, lambda e: forward(0, e))
-    forward(1, 2)
-    forward(1, 12)
-    over(4, 4, lambda e: forward(1, e))
-
-    all_pred[mem] = own_pred[...]
-    pred_copies = [
-        send(own_pred, all_pred.at[mem], mem_sems, step, device) for step, (device, _) in enumerate(members)
-    ]
-    predictions[...] = own_pred[:, pl.ds(0, 2)]
+    over(6, 2, lambda e: forward(1, e))
+    over_rows(0, HALO, make_noise)
+    over_rows(HALO + ROWS, HALO, make_noise)
+    wait(near_copies)
+    for e in (2, 3, 12, 13):
+        entry(e)
+    for b, e in ((0, 3), (0, 11), (1, 4), (1, 10)):
+        forward(b, e)
+    own_copies = share(0, 2, mem_sems.at[0])
     for v in range(2):
+        for m in range(HERE):
+            predictions[m, v] = own_pred[v, m]
         target_tiles[v] = targets[v]
         for side in range(2):
             target_tiles[2, pl.ds(4 * v + 2 * side, 2), :] = edge_in[side, pl.ds(2 * v, 2), :]
             weight_tiles[1, pl.ds(4 * v + 2 * side, 2), :] = edge_in[side, pl.ds(4, 2), :]
     weight_tiles[0] = land_mask[...].astype(F32)
+    wait(far_copies)
+    for e in (0, 1, 14, 15):
+        entry(e)
+    for b, e in ((0, 1), (0, 13), (1, 2), (1, 12)):
+        forward(b, e)
+    edge_copies = share(2, 1, mem_sems.at[1])
+
     own_row = lax.broadcasted_iota(jnp.int32, (8, COLS), 0)
     side_row = own_row % 4
     side_row = jnp.where(side_row < 2, side_row - 2, side_row + ROWS - 2)
     for at, rows in enumerate((own_row, side_row)):
         area = 1.0 - 2.0 * (rows + tile * ROWS).astype(F32) / (3.0 * GRID_ROWS)
         weight_tiles[at] = area * (1.0 + weight_tiles[at])
-    wait(pred_copies)
-
-    def lengths(own, edge):
-        squares = edge * edge
-        return own[0] * own[0] + own[1] * own[1] + smooth_sq, squares + pltpu.roll(squares, 4, axis=0) + smooth_sq
 
     cells = GRID_ROWS * COLS
-    loss_tile = jnp.zeros((8, COLS), F32)
-    for m in range(HERE):
-        mine = [own_pred[m, part] for part in range(3)]
-
-        def pull_from(n, carry):
-            pulls, total = carry
-            gaps = [mine[part] - all_pred[n // HERE, lax.rem(n, HERE), part] for part in range(3)]
-            own_sq, edge_sq = lengths(gaps[:2], gaps[2])
-            own_inv, edge_inv = lax.rsqrt(own_sq), lax.rsqrt(edge_sq)
-            pulls = tuple(
-                pull + gap * inv for pull, gap, inv in zip(pulls, gaps, (own_inv, own_inv, edge_inv))
+
+    def length_sq(gaps):
+        if len(gaps) == 2:
+            return gaps[0] * gaps[0] + gaps[1] * gaps[1] + smooth_sq
+        squares = gaps[0] * gaps[0]
+        return squares + pltpu.roll(squares, 4, axis=0) + smooth_sq
+
+    def pull_apart(m, parts_here, weights):
+        mine = [own_pred[part, m] for part in parts_here]
+        pulls = [jnp.zeros((8, COLS), F32) for _ in parts_here]
+        total = jnp.zeros((8, COLS), F32) - smooth_sq**0.5
+        for n in range(MEMBERS):
+            gaps = [own - all_pred[n // HERE, part, n % HERE] for own, part in zip(mine, parts_here)]
+            square = length_sq(gaps)
+            inverse = lax.rsqrt(square)
+            pulls = [pull + gap * inverse for pull, gap in zip(pulls, gaps)]
+            total = total + square * inverse
+        misses = [own - target_tiles[part] for own, part in zip(mine, parts_here)]
+        square = length_sq(misses)
+        inverse = lax.rsqrt(square)
+        factor = weights * (LOSS_SCALE / cells)
+        for part, miss, pull in zip(parts_here, misses, pulls):
+            grad = factor * (
+                miss * inverse * (1.0 / MEMBERS) - pull * (1.0 / (MEMBERS * (MEMBERS - 1.0)))
             )
-            return pulls, total + own_sq * own_inv
-
-        blank_tile = jnp.zeros((8, COLS), F32)
-        pulls, total = lax.fori_loop(0, MEMBERS, pull_from, ((blank_tile,) * 3, blank_tile - smooth_sq**0.5))
-        misses = [mine[part] - target_tiles[part] for part in range(3)]
-        own_sq, edge_sq = lengths(misses[:2], misses[2])
-        own_inv, edge_inv = lax.rsqrt(own_sq), lax.rsqrt(edge_sq)
-        loss_tile += weight_tiles[0] * (
-            own_sq * own_inv * (1.0 / MEMBERS) - total * (1.0 / (2.0 * MEMBERS * (MEMBERS - 1)))
+            pred_grad[part, m] = grad.astype(BF16).astype(F32)
+        return weights * (
+            square * inverse * (1.0 / MEMBERS) - total * (1.0 / (2.0 * MEMBERS * (MEMBERS - 1)))
         )
-        for part, inv in enumerate((own_inv, own_inv, edge_inv)):
-            factor = weight_tiles[part // 2] * (LOSS_SCALE / cells)
-            grad = factor * (
-                misses[part] * inv * (1.0 / MEMBERS) - pulls[part] * (1.0 / (MEMBERS * (MEMBERS - 1.0)))
-            )
-            pred_grad[m, part] = grad.astype(BF16).astype(F32)
 
     def top(e, own):
         for m in range(HERE):
             (part0, at0), (part1, at1) = spots(e)
-            pull0 = pred_grad[m, part0, pl.ds(at0, 1), :]
-            pull1 = pred_grad[m, part1, pl.ds(at1, 1), :]
+            pull0 = pred_grad[part0, m, pl.ds(at0, 1), :]
+            pull1 = pred_grad[part1, m, pl.ds(at1, 1), :]
             grad = gains[3] * pull0 + gains[4] * pull1
             inverse = inverse2[e, m, pl.ds(0, 1), :]
             normed = stream2[e, m] * inverse
@@ -392,18 +445,17 @@
             stream_grad[e, m] = grad
             grads1[e, m] = (grad * (slope1[e, m] * inside(e))).astype(BF16)
 
-    def tap_grads(grads, inputs):
-        tap_sum[...] = jnp.zeros_like(tap_sum)
-
-        def one(e):
+    def tap_grads(b, rows, fresh):
+        grads, inputs = ((grads0, inputs0), (grads1, inputs1))[b]
+        shifted, windows = [], []
+        for e in rows:
             for m in range(HERE):
-                grad = grads[e, m].astype(F32)
-                shifts = [from_right(grad), grad, from_left(grad)]
-                shifts = jnp.concatenate([shift.astype(BF16) for shift in shifts], axis=0)
-                window = inputs[pl.ds(e - 1, 3), m].reshape(3 * CH, COLS)
-                tap_sum[:, pl.ds(0, 3 * CH)] += dot_rows(shifts, window)
-
-        over_rows(HALO, ROWS, one)
+                grad = grads[e, m]
+                shifted.append(jnp.concatenate([from_right(grad), grad, from_left(grad)], axis=0))
+                windows.append(inputs[pl.ds(e - 1, 3), m].reshape(3 * CH, COLS))
+        found = dot_rows(jnp.concatenate(shifted, axis=1), jnp.concatenate(windows, axis=1))
+        at = pl.ds(0, 3 * CH)
+        tap_sum[b, :, at] = found if fresh else tap_sum[b, :, at] + found
 
     def backward(b, e, last):
         source, stream, inverses = ((grads0, stream0, inverse0), (grads1, stream1, inverse1))[b]
@@ -415,8 +467,9 @@
                 grad = middle + from_right(left) + from_left(right)
                 inverse = inverses[e + ro, m, pl.ds(0, 1), :]
                 normed = stream[e + ro, m] * inverse
-                counted = jnp.where((e + ro >= HALO) & (e + ro < HALO + ROWS), 1.0, 0.0).astype(F32)
-                sums[b] += grad * (normed * counted)
+                counted = HALO <= e + ro < HALO + ROWS
+                if counted:
+                    sums[b] += grad * normed
                 total = stream_grad[e + ro, m] + norm_back(grad * gains[b], normed, inverse)
                 if b == 1:
                     stream_grad[e + ro, m] = total
@@ -426,56 +479,61 @@
 
     def to_parts(b):
         for at in range(GROUP):
-            parts[b, at] = tap_sum[pl.ds(CHUNK * (at // 2), CHUNK), pl.ds(128 * (at % 2), 128)]
+            parts[b, at] = tap_sum[b, pl.ds(CHUNK * (at // 2), CHUNK), pl.ds(128 * (at % 2), 128)]
 
     def scatter(b):
         return [
             send(parts.at[b, rank], scattered.at[b, step], plane_sems.at[b], step, device)
-            for step, (device, rank) in enumerate(plane)
+            for step, (device, rank) in enumerate(groups[b][0])
         ]
 
     def spread_out(b):
-        total = parts[b, in_plane]
+        in_first, in_second = ranks[b]
+        total = parts[b, in_first]
         for step in range(GROUP - 1):
             total = total + scattered[b, step]
-        spread[b, in_line] = total
+        spread[b, in_second] = total
         return [
-            send(spread.at[b, in_line], spread.at[b, in_line], line_sems.at[b], step, device)
-            for step, (device, _) in enumerate(line)
+            send(spread.at[b, in_second], spread.at[b, in_second], line_sems.at[b], step, device)
+            for step, (device, _) in enumerate(groups[b][1])
         ]
 
     def gather(b):
         total = spread[b, 0]
         for rank in range(1, GROUP):
             total = total + spread[b, rank]
-        gathered[b, in_plane] = total
+        in_first = ranks[b][0]
+        gathered[b, in_first] = total
         return [
-            send(gathered.at[b, in_plane], gathered.at[b, in_plane], back_sems.at[b], step, device)
-            for step, (device, _) in enumerate(plane)
+            send(gathered.at[b, in_first], gathered.at[b, in_first], back_sems.at[b], step, device)
+            for step, (device, _) in enumerate(groups[b][0])
         ]
 
-    def finish(b):
-        for at in range(GROUP):
-            whole[pl.ds(CHUNK * (at // 2), CHUNK), pl.ds(128 * (at % 2), 128)] = gathered[b, at]
-        for dr in range(3):
-            for dc in range(3):
-                grad_conv[b, 3 * dr + dc] = whole[pl.ds(CH * dc, CH), pl.ds(CH * dr, CH)]
-
+    wait(own_copies)
+    loss_tile = jnp.zeros((8, COLS), F32)
+    for m in range(HERE):
+        loss_tile += pull_apart(m, (0, 1), weight_tiles[0])
+    over_rows(HALO, ROWS, lambda e: top(e, True))
+    tap_grads(1, range(HALO, HALO + ROWS), True)
+    to_parts(1)
+    first_1 = scatter(1)
+    over(5, 3, lambda e: backward(1, e, None))
+    tap_grads(0, range(5, 11), True)
+    wait(edge_copies)
+    for m in range(HERE):
+        pull_apart(m, (2,), weight_tiles[1])
     for e in (2, 3, 12, 13):
         top(e, False)
-    over_rows(HALO, ROWS, lambda e: top(e, True))
-    tap_grads(grads1, inputs1)
-    to_parts(1)
-    plane_1 = scatter(1)
-    over(3, 5, lambda e: backward(1, e, None))
-    tap_grads(grads0, inputs0)
+    for e in (3, 11):
+        backward(1, e, None)
+    tap_grads(0, (4, 11), False)
     to_parts(0)
-    plane_0 = scatter(0)
-    wait(plane_1)
-    line_1 = spread_out(1)
+    first_0 = scatter(0)
+    wait(first_1)
+    second_1 = spread_out(1)
 
     small[...] = jnp.zeros_like(small)
-    sum_noise = tap_sum.at[pl.ds(0, CH), pl.ds(0, NOISE)]
+    sum_noise = tap_sum.at[0, pl.ds(0, CH), pl.ds(0, NOISE)]
     sum_noise[...] = jnp.zeros((CH, NOISE), F32)
 
     def last(e, m, entry_grad):
@@ -495,9 +553,9 @@
     small_1 = [
         send(small, small_in.at[in_plane], small_sems, step, device) for step, (device, _) in enumerate(plane)
     ]
-    wait(plane_0)
-    line_0 = spread_out(0)
-    wait(line_1)
+    wait(first_0)
+    second_0 = spread_out(0)
+    wait(second_1)
     back_1 = gather(1)
     wait(small_1)
     total = small_in[0]
@@ -508,17 +566,30 @@
         send(small_line.at[in_line], small_line.at[in_line], small_line_sems, step, device)
         for step, (device, _) in enumerate(line)
     ]
-    wait(line_0)
+    wait(second_0)
     back_0 = gather(0)
     wait(back_1)
-    finish(1)
     wait(small_2)
     total = small_line[0]
     for rank in range(1, GROUP):
         total = total + small_line[rank]
     small_out[...] = total
     wait(back_0)
-    finish(0)
+
+
+def unpack_kernel(
+    predictions, gathered, small, loss, pred_out, grad_conv, grad_gain, grad_head, grad_head_gain, grad_noise, whole
+):
+    pred_out[...] = predictions[...]
+    for b in range(2):
+        for at in range(GROUP):
+            whole[pl.ds(CHUNK * (at // 2), CHUNK), pl.ds(128 * (at % 2), 128)] = gathered[b, at]
+        for dr in range(3):
+            for dc in range(3):
+                grad_conv[b, 3 * dr + dc] = whole[pl.ds(CH * dc, CH), pl.ds(CH * dr, CH)]
+    for out, first, count in ((grad_gain, 0, 2), (grad_head_gain, 2, 1), (grad_head, 3, 2), (grad_noise, 5, NOISE)):
+        out[...] = small[pl.ds(first, count), pl.ds(0, CH)]
+    loss[...] = small[pl.ds(13, 1), pl.ds(0, 1)]
 
 
 def on_device(
@@ -533,7 +604,7 @@
     head_gain,
 ):
     vmem = pl.BlockSpec(memory_space=pltpu.VMEM)
-    smem = pl.BlockSpec(memory_space=pltpu.SMEM)
+    far = pl.BlockSpec(memory_space=pltpu.HBM)
 
     def field(*shape):
         return pltpu.VMEM((EXT, HERE) + shape, F32)
@@ -545,6 +616,16 @@
         return pltpu.SemaphoreType.DMA(shape)
 
     scratch = dict(
+        block_input=pltpu.VMEM(block_input.shape, BF16),
+        seeds=pltpu.SMEM(member_seeds.shape, jnp.int32),
+        targets=pltpu.VMEM(targets.shape, F32),
+        land_mask=pltpu.VMEM(land_mask.shape, jnp.int32),
+        noise_weight=pltpu.VMEM((NOISE, CH), BF16),
+        conv_weight=pltpu.VMEM(conv_weight.shape, BF16),
+        block_gain=pltpu.VMEM(block_gain.shape, F32),
+        head_weight=pltpu.VMEM(head_weight.shape, BF16),
+        head_gain=pltpu.VMEM((1, CH), F32),
+        load_sems=sems(9),
         turned=pltpu.VMEM((HERE, 2, CH * ROWS, 128), F32),
         raw=half(CH, COLS),
         noise=field(NOISE, COLS),
@@ -564,44 +645,43 @@
         head_in=half(CH, COLS),
         forward_taps=pltpu.VMEM((2, 6 * CH, 4 * CH), BF16),
         backward_taps=pltpu.VMEM((2, 6 * CH, 4 * CH), BF16),
+        noise_taps=pltpu.VMEM((CH, NOISE), BF16),
         gains=pltpu.VMEM((5, CH, COLS), F32),
         edge_out=pltpu.VMEM((2, 8, COLS), F32),
         edge_in=pltpu.VMEM((2, 8, COLS), F32),
         target_tiles=pltpu.VMEM((3, 8, COLS), F32),
         weight_tiles=pltpu.VMEM((2, 8, COLS), F32),
-        own_pred=pltpu.VMEM((HERE, 3, 8, COLS), F32),
-        all_pred=pltpu.VMEM((MEMS, HERE, 3, 8, COLS), F32),
-        pred_grad=pltpu.VMEM((HERE, 3, 8, COLS), F32),
+        own_pred=pltpu.VMEM((3, HERE, 8, COLS), F32),
+        all_pred=pltpu.VMEM((MEMS, 3, HERE, 8, COLS), F32),
+        pred_grad=pltpu.VMEM((3, HERE, 8, COLS), F32),
         sums=pltpu.VMEM((5, CH, COLS), F32),
-        tap_sum=pltpu.VMEM((3 * CH, 256), F32),
+        tap_sum=pltpu.VMEM((2, 3 * CH, 256), F32),
         parts=pltpu.VMEM((2, GROUP, CHUNK, 128), F32),
         scattered=pltpu.VMEM((2, GROUP - 1, CHUNK, 128), F32),
         spread=pltpu.VMEM((2, GROUP, CHUNK, 128), F32),
-        gathered=pltpu.VMEM((2, GROUP, CHUNK, 128), F32),
-        whole=pltpu.VMEM((3 * CH, 256), F32),
         small=pltpu.VMEM((16, 128), F32),
         small_in=pltpu.VMEM((GROUP, 16, 128), F32),
         small_line=pltpu.VMEM((GROUP, 16, 128), F32),
-        halo_sems=sems(2, 4),
-        mem_sems=sems(2, MEMS - 1),
+        halo_sems=sems(2, 6),
+        mem_sems=sems(2, 2, MEMS - 1),
         plane_sems=sems(2, 2, GROUP - 1),
         line_sems=sems(2, 2, GROUP - 1),
         back_sems=sems(2, 2, GROUP - 1),
         small_sems=sems(2, GROUP - 1),
         small_line_sems=sems(2, GROUP - 1),
     )
-    predictions, grad_conv, small = pl.pallas_call(
+    predictions, gathered, small = pl.pallas_call(
         step_kernel,
         out_shape=(
             jax.ShapeDtypeStruct((HERE, 2, ROWS, COLS), F32),
-            jax.ShapeDtypeStruct((2, 9, CH, CH), F32),
+            jax.ShapeDtypeStruct((2, GROUP, CHUNK, 128), F32),
             jax.ShapeDtypeStruct((16, 128), F32),
         ),
-        in_specs=[vmem, smem] + [vmem] * 7,
+        in_specs=[far] * 9,
         out_specs=(vmem, vmem, vmem),
         scratch_shapes=list(scratch.values()),
         compiler_params=pltpu.CompilerParams(
-            collective_id=0, has_side_effects=True, vmem_limit_bytes=48 * 2**20
+            collective_id=0, has_side_effects=True, vmem_limit_bytes=VMEM_BYTES
         ),
         name="train_step",
     )(
@@ -609,20 +689,37 @@
         member_seeds,
         targets,
         land_mask,
-        noise_weight,
+        noise_weight.T,
         conv_weight,
         block_gain,
         head_weight,
         head_gain.reshape(1, CH),
     )
+    loss, predictions, grad_conv, grad_block_gain, grad_head_weight, grad_head_gain, grad_noise = pl.pallas_call(
+        unpack_kernel,
+        out_shape=(
+            jax.ShapeDtypeStruct((1, 1), F32),
+            jax.ShapeDtypeStruct((HERE, 2, ROWS, COLS), F32),
+            jax.ShapeDtypeStruct((2, 9, CH, CH), F32),
+            jax.ShapeDtypeStruct((2, CH), F32),
+            jax.ShapeDtypeStruct((2, CH), F32),
+            jax.ShapeDtypeStruct((1, CH), F32),
+            jax.ShapeDtypeStruct((NOISE, CH), F32),
+        ),
+        in_specs=[vmem] * 3,
+        out_specs=(vmem,) * 7,
+        scratch_shapes=[pltpu.VMEM((3 * CH, 256), F32)],
+        compiler_params=pltpu.CompilerParams(vmem_limit_bytes=VMEM_BYTES),
+        name="unpack",
+    )(predictions, gathered, small)
     return (
-        small[13, 0],
+        loss.reshape(()),
         predictions,
         grad_conv,
-        small[0:2, :CH],
-        small[3:5, :CH],
-        small[2, :CH],
-        small[5:13, :CH].T,
+        grad_block_gain,
+        grad_head_weight,
+        grad_head_gain.reshape(CH),
+        grad_noise.T,
     )
 
 

time: 73.3 us -> 58.5 us (0.80)
  Pallas kernels: 65.2 us -> 57.7 us
  local copies, waits for them, and re-layouts: 7.14 us -> 0 us
    pallas_call x1, Pallas kernels: 65.2 us -> 55.8 us  [on_device(): pl.pallas_call(step_kernel, out_shape=(jax.ShapeDtypeStruct((HERE, 2, ROW...]
    unnamed x19 -> x0, local copies, waits for them, and re-layouts: 4.95 us -> none
    pallas_call x0 -> x1, Pallas kernels: none -> 1.94 us  [on_device(): pl.pallas_call(unpack_kernel, out_shape=(jax.ShapeDtypeStruct((1, 1), F32...]
    slice x2 -> x0, local copies, waits for them, and re-layouts: 1.08 us -> none  [the longest x1 0.57 us: on_device(): small[3:5, :CH]]
where the time goes in v3:
time: 58.5 us; the launch traced here: 58.4 us
  Pallas kernels  57.7 us (99%)
  between operations  0.64 us (1%)
    pallas_call x1, Pallas kernels, on_device(): pl.pallas_call(step_kernel, out_shape=(jax.ShapeDtypeStruct((HERE, 2, ROW...  55.8 us
    pallas_call x1, Pallas kernels, on_device(): pl.pallas_call(unpack_kernel, out_shape=(jax.ShapeDtypeStruct((1, 1), F32...  1.94 us

profile of v3, /device:TPU:1, one launch (start us, length us, event | category | flops | bytes accessed | tf_op | source)
XLA Modules:
  0.0 58.4 jit_solution(8290542675448535809)
XLA Ops:
  0.6 55.8 %train_step.1 = (f32[2,2,8,256]{3,2,1,0:T(8,128)}, f32[2,16,24,128]{3,2,1,0:T(8,128)}, f32[16,128]{1,0:T(8,128)}) custom-call(bf16[2,64,8,256]{3,2,1,0:T(8,128)(2,1)} %block_input_far.1, s32[2]{0:T(128)} %seeds_far.1, f32[2,8,256]{2,1,0:T(8,128)} %targets_far.1, s32[8,256]{1,0:T(8,128)} %land_mask_far.1, bf16[8,64]{1,0:T(8,128)(2,1)} %bitcast.5, ...), custom_call_target="tpu_custom_call" | custom-call | tf_op jit(solution)/shard_map/train_step/pallas_call | solution.py:673
  56.4 1.9 %unpack.1 = (f32[1,1]{1,0:T(1,128)}, f32[2,2,8,256]{3,2,1,0:T(8,128)}, f32[2,9,64,64]{3,2,1,0:T(8,128)}, f32[2,64]{1,0:T(2,128)}, f32[2,64]{1,0:T(2,128)}, /*index=5*/f32[1,64]{1,0:T(1,128)}, f32[8,64]{1,0:T(8,128)}) custom-call(f32[2,2,8,256]{3,2,1,0:T(8,128)} %get-tuple-element.17.predictions, f32[2,16,24,128]{3,2,1,0:T(8,128)} %get-tuple-element.18.gathered, ...), custom_call_target="tpu_custom_call" | custom-call | tf_op jit(solution)/shard_map/unpack/pallas_call | solution.py:698

commit v4 on v3

--- a/solution.py
+++ b/solution.py
@@ -19,7 +19,8 @@
 HALO = 4
 EXT = ROWS + 2 * HALO
 GRID_ROWS = ROWS * TILES
-CHUNK = 24
+PART = 6
+DEPTH = 8
 VMEM_BYTES = 63 * 2**20
 F32 = jnp.float32
 BF16 = jnp.bfloat16
@@ -46,14 +47,14 @@
     return device_at(rank // 4, rank % 4, z, core)
 
 
-def line_rank():
-    _, _, z, core = coordinates()
-    return z * 2 + core
-
-
-def line_device(rank):
-    x, y, _, _ = coordinates()
-    return device_at(x, y, rank // 2, rank % 2)
+def depth_device(rank):
+    x, y, _, core = coordinates()
+    return device_at(x, y, rank, core)
+
+
+def core_device(rank):
+    x, y, z, _ = coordinates()
+    return device_at(x, y, z, rank)
 
 
 def mem_device(rank):
@@ -186,13 +187,16 @@
     sums,
     tap_sum,
     parts,
+    core_in,
     scattered,
     spread,
     small,
+    small_core,
     small_in,
     small_line,
     halo_sems,
     mem_sems,
+    core_sems,
     plane_sems,
     line_sems,
     back_sems,
@@ -200,11 +204,12 @@
     small_line_sems,
 ):
     mem, tile = lax.axis_index("mem"), lax.axis_index("tile")
-    in_plane, in_line = plane_rank(), line_rank()
+    in_plane = plane_rank()
+    _, _, depth, core = coordinates()
+    other_core = 1 - core
     below, above = lax.rem(tile + 1, TILES), lax.rem(tile + TILES - 1, TILES)
     plane = [(plane_device(rank), rank) for rank in others(in_plane, GROUP)]
-    line = [(line_device(rank), rank) for rank in others(in_line, GROUP)]
-    groups, ranks = ((plane, line), (line, plane)), ((in_plane, in_line), (in_line, in_plane))
+    line = [(depth_device(rank), rank) for rank in others(depth, DEPTH)]
     members = [(mem_device(rank), rank) for rank in others(mem, MEMS)]
 
     loads = [
@@ -227,7 +232,9 @@
         load.start()
 
     barrier = pltpu.get_barrier_semaphore()
-    for device in [(mem, below), (mem, above)] + [d for d, _ in plane + line + members]:
+    for device in [(mem, below), (mem, above)] + [core_device(other_core)] + [
+        d for d, _ in plane + line + members
+    ]:
         pl.semaphore_signal(barrier, inc=1, device_id=device, device_id_type=MESH_ID)
 
     def send(source, target, sems, slot, device):
@@ -246,33 +253,41 @@
         for copy in copies:
             copy.wait()
 
-    wait(loads)
+    loads[0].wait()
     for m in range(HERE):
         for half in range(2):
             lanes = pl.ds(128 * half, 128)
             turned[m, half] = block_input[m, :, :, lanes].astype(F32).reshape(CH * ROWS, 128)
-            for r in range(ROWS):
-                raw[HALO + r, m, :, lanes] = turned[m, half, pl.ds(r, CH, stride=ROWS), :].astype(BF16)
+
+    def bring(rows):
+        for r in rows:
+            for m in range(HERE):
+                for half in range(2):
+                    lanes = pl.ds(128 * half, 128)
+                    raw[HALO + r, m, :, lanes] = turned[m, half, pl.ds(r, CH, stride=ROWS), :].astype(BF16)
+
+    bring((0, 1, 6, 7))
+    pl.semaphore_wait(barrier, 3 + (GROUP - 1) + (DEPTH - 1) + (MEMS - 1))
+
+    def halo(up, down, up_to, down_to, slot):
+        return [
+            send(raw.at[pl.ds(up, 2)], raw.at[pl.ds(up_to, 2)], halo_sems, slot, (mem, above)),
+            send(raw.at[pl.ds(down, 2)], raw.at[pl.ds(down_to, 2)], halo_sems, slot + 1, (mem, below)),
+        ]
+
+    near_copies = halo(4, 10, 12, 2, 0)
+    bring(range(2, 6))
+    far_copies = halo(6, 8, 14, 0, 2)
+    wait(loads[1:])
     for side, start in ((0, 0), (1, ROWS - 2)):
         edge_out[side] = jnp.zeros((8, COLS), F32)
         for v in range(2):
             edge_out[side, pl.ds(2 * v, 2), :] = targets[v, pl.ds(start, 2), :]
         edge_out[side, pl.ds(4, 2), :] = land_mask[pl.ds(start, 2), :].astype(F32)
-
-    pl.semaphore_wait(barrier, 2 + 2 * (GROUP - 1) + (MEMS - 1))
-
-    def halo(up, down, up_to, down_to, slot):
-        return [
-            send(raw.at[pl.ds(up, 2)], raw.at[pl.ds(up_to, 2)], halo_sems, slot, (mem, above)),
-            send(raw.at[pl.ds(down, 2)], raw.at[pl.ds(down_to, 2)], halo_sems, slot + 1, (mem, below)),
-        ]
-
-    near_copies = halo(4, 10, 12, 2, 0)
-    near_copies += [
+    far_copies += [
         send(edge_out.at[0], edge_in.at[1], halo_sems, 4, (mem, above)),
         send(edge_out.at[1], edge_in.at[0], halo_sems, 5, (mem, below)),
     ]
-    far_copies = halo(6, 8, 14, 0, 2)
 
     unit = diagonal().astype(F32).astype(BF16)
     blank = jnp.zeros((CH, CH), BF16)
@@ -294,6 +309,7 @@
     for at in range(5):
         sums[at] = jnp.zeros((CH, COLS), F32)
     tap_sum[...] = jnp.zeros_like(tap_sum)
+    parts[...] = jnp.zeros_like(parts)
 
     def inside(e):
         row = tile * ROWS - HALO + e
@@ -338,10 +354,11 @@
                     place(own_pred, m, e + ro, found)
 
     def spots(e):
-        if isinstance(e, int) and not HALO <= e < HALO + ROWS:
-            at = (e - 2) if e < HALO else (e - HALO - ROWS + 2)
-            return [(2, at), (2, at + 4)]
-        return [(0, e - HALO), (1, e - HALO)]
+        if 6 <= e < 10:
+            return [(0, e - 6), (0, e - 2)]
+        part = 1 if HALO <= e < HALO + ROWS else 2
+        at = e - HALO + 2 * part - 2 if e < 8 else e - HALO - ROWS + 6 - 2 * part
+        return [(part, at), (part, at + 4)]
 
     def place(ref, m, e, pair):
         for v, (part, at) in enumerate(spots(e)):
@@ -355,11 +372,10 @@
         for i in range(count):
             body(first + i)
 
-    def share(first, count, sems):
-        parts_here = pl.ds(first, count)
-        all_pred[mem, parts_here] = own_pred[parts_here]
+    def share(part):
+        all_pred[mem, part] = own_pred[part]
         return [
-            send(own_pred.at[parts_here], all_pred.at[mem, parts_here], sems, step, device)
+            send(own_pred.at[part], all_pred.at[mem, part], mem_sems.at[part], step, device)
             for step, (device, _) in enumerate(members)
         ]
 
@@ -367,63 +383,67 @@
     over_rows(HALO, ROWS, entry)
     over(5, 3, lambda e: forward(0, e))
     over(6, 2, lambda e: forward(1, e))
+    shared = [share(0)]
     over_rows(0, HALO, make_noise)
     over_rows(HALO + ROWS, HALO, make_noise)
+    for v in range(2):
+        target_tiles[0, pl.ds(4 * v, 4), :] = targets[v, pl.ds(2, 4), :]
+        weight_tiles[0, pl.ds(4 * v, 4), :] = land_mask[pl.ds(2, 4), :].astype(F32)
+        for side in range(2):
+            at = pl.ds(4 * v + 2 * side, 2)
+            target_tiles[1, at, :] = targets[v, pl.ds(6 * side, 2), :]
+            weight_tiles[1, at, :] = land_mask[pl.ds(6 * side, 2), :].astype(F32)
     wait(near_copies)
     for e in (2, 3, 12, 13):
         entry(e)
     for b, e in ((0, 3), (0, 11), (1, 4), (1, 10)):
         forward(b, e)
-    own_copies = share(0, 2, mem_sems.at[0])
-    for v in range(2):
-        for m in range(HERE):
-            predictions[m, v] = own_pred[v, m]
-        target_tiles[v] = targets[v]
-        for side in range(2):
-            target_tiles[2, pl.ds(4 * v + 2 * side, 2), :] = edge_in[side, pl.ds(2 * v, 2), :]
-            weight_tiles[1, pl.ds(4 * v + 2 * side, 2), :] = edge_in[side, pl.ds(4, 2), :]
-    weight_tiles[0] = land_mask[...].astype(F32)
+    shared.append(share(1))
     wait(far_copies)
     for e in (0, 1, 14, 15):
         entry(e)
     for b, e in ((0, 1), (0, 13), (1, 2), (1, 12)):
         forward(b, e)
-    edge_copies = share(2, 1, mem_sems.at[1])
-
-    own_row = lax.broadcasted_iota(jnp.int32, (8, COLS), 0)
-    side_row = own_row % 4
-    side_row = jnp.where(side_row < 2, side_row - 2, side_row + ROWS - 2)
-    for at, rows in enumerate((own_row, side_row)):
+    shared.append(share(2))
+    for v in range(2):
+        for m in range(HERE):
+            predictions[m, v, pl.ds(2, 4), :] = own_pred[0, m, pl.ds(4 * v, 4), :]
+            for side in range(2):
+                predictions[m, v, pl.ds(6 * side, 2), :] = own_pred[1, m, pl.ds(4 * v + 2 * side, 2), :]
+        for side in range(2):
+            at = pl.ds(4 * v + 2 * side, 2)
+            target_tiles[2, at, :] = edge_in[side, pl.ds(2 * v, 2), :]
+            weight_tiles[2, at, :] = edge_in[side, pl.ds(4, 2), :]
+    place_in = lax.broadcasted_iota(jnp.int32, (8, COLS), 0) % 4
+    for part, (first, second) in enumerate(((2, 4), (0, 6), (-2, 8))):
+        rows = jnp.where(place_in < 2, place_in + first, place_in - 2 + second)
         area = 1.0 - 2.0 * (rows + tile * ROWS).astype(F32) / (3.0 * GRID_ROWS)
-        weight_tiles[at] = area * (1.0 + weight_tiles[at])
+        weight_tiles[part] = area * (1.0 + weight_tiles[part])
 
     cells = GRID_ROWS * COLS
 
-    def length_sq(gaps):
-        if len(gaps) == 2:
-            return gaps[0] * gaps[0] + gaps[1] * gaps[1] + smooth_sq
-        squares = gaps[0] * gaps[0]
-        return squares + pltpu.roll(squares, 4, axis=0) + smooth_sq
-
-    def pull_apart(m, parts_here, weights):
-        mine = [own_pred[part, m] for part in parts_here]
-        pulls = [jnp.zeros((8, COLS), F32) for _ in parts_here]
+    def length_sq(gap):
+        square = gap * gap
+        return square + pltpu.roll(square, 4, axis=0) + smooth_sq
+
+    def pull_apart(m, part):
+        mine = own_pred[part, m]
+        pull = jnp.zeros((8, COLS), F32)
         total = jnp.zeros((8, COLS), F32) - smooth_sq**0.5
         for n in range(MEMBERS):
-            gaps = [own - all_pred[n // HERE, part, n % HERE] for own, part in zip(mine, parts_here)]
-            square = length_sq(gaps)
+            gap = mine - all_pred[n // HERE, part, n % HERE]
+            square = length_sq(gap)
             inverse = lax.rsqrt(square)
-            pulls = [pull + gap * inverse for pull, gap in zip(pulls, gaps)]
+            pull = pull + gap * inverse
             total = total + square * inverse
-        misses = [own - target_tiles[part] for own, part in zip(mine, parts_here)]
-        square = length_sq(misses)
+        miss = mine - target_tiles[part]
+        square = length_sq(miss)
         inverse = lax.rsqrt(square)
-        factor = weights * (LOSS_SCALE / cells)
-        for part, miss, pull in zip(parts_here, misses, pulls):
-            grad = factor * (
-                miss * inverse * (1.0 / MEMBERS) - pull * (1.0 / (MEMBERS * (MEMBERS - 1.0)))
-            )
-            pred_grad[part, m] = grad.astype(BF16).astype(F32)
+        weights = weight_tiles[part]
+        grad = (weights * (LOSS_SCALE / cells)) * (
+            miss * inverse * (1.0 / MEMBERS) - pull * (1.0 / (MEMBERS * (MEMBERS - 1.0)))
+        )
+        pred_grad[part, m] = grad.astype(BF16).astype(F32)
         return weights * (
             square * inverse * (1.0 / MEMBERS) - total * (1.0 / (2.0 * MEMBERS * (MEMBERS - 1)))
         )
@@ -477,60 +497,74 @@
                 else:
                     last(e + ro, m, total.astype(BF16))
 
-    def to_parts(b):
-        for at in range(GROUP):
-            parts[b, at] = tap_sum[b, pl.ds(CHUNK * (at // 2), CHUNK), pl.ds(128 * (at % 2), 128)]
-
-    def scatter(b):
+    def across(source, target, sems, slot):
+        return [send(source, target, sems, slot, core_device(other_core))]
+
+    def to_core(b):
+        for half in range(2):
+            for at in range(GROUP):
+                rows = pl.ds(PART * (GROUP * half + at), PART)
+                parts[b, half, at, pl.ds(0, PART), :] = tap_sum[b, rows, :]
+        return across(parts.at[b, other_core], core_in.at[b], core_sems, b)
+
+    def to_plane(b):
+        parts[b, core] = parts[b, core] + core_in[b]
         return [
-            send(parts.at[b, rank], scattered.at[b, step], plane_sems.at[b], step, device)
-            for step, (device, rank) in enumerate(groups[b][0])
+            send(parts.at[b, core, rank], scattered.at[b, step], plane_sems.at[b], step, device)
+            for step, (device, rank) in enumerate(plane)
         ]
 
-    def spread_out(b):
-        in_first, in_second = ranks[b]
-        total = parts[b, in_first]
+    def to_depth(b):
+        total = parts[b, core, in_plane]
         for step in range(GROUP - 1):
             total = total + scattered[b, step]
-        spread[b, in_second] = total
+        spread[b, depth] = total
         return [
-            send(spread.at[b, in_second], spread.at[b, in_second], line_sems.at[b], step, device)
-            for step, (device, _) in enumerate(groups[b][1])
+            send(spread.at[b, depth], spread.at[b, depth], line_sems.at[b], step, device)
+            for step, (device, _) in enumerate(line)
         ]
 
-    def gather(b):
+    def to_plane_again(b):
         total = spread[b, 0]
-        for rank in range(1, GROUP):
+        for rank in range(1, DEPTH):
             total = total + spread[b, rank]
-        in_first = ranks[b][0]
-        gathered[b, in_first] = total
-        return [
-            send(gathered.at[b, in_first], gathered.at[b, in_first], back_sems.at[b], step, device)
-            for step, (device, _) in enumerate(groups[b][0])
-        ]
-
-    wait(own_copies)
-    loss_tile = jnp.zeros((8, COLS), F32)
-    for m in range(HERE):
-        loss_tile += pull_apart(m, (0, 1), weight_tiles[0])
-    over_rows(HALO, ROWS, lambda e: top(e, True))
-    tap_grads(1, range(HALO, HALO + ROWS), True)
-    to_parts(1)
-    first_1 = scatter(1)
-    over(5, 3, lambda e: backward(1, e, None))
+        gathered[b, core, in_plane] = total
+        mine = gathered.at[b, core, in_plane]
+        return [send(mine, mine, back_sems.at[b], step, device) for step, (device, _) in enumerate(plane)]
+
+    def to_core_again(b):
+        return across(gathered.at[b, core], gathered.at[b, core], core_sems, 2 + b)
+
+    def grads_of(part):
+        found = jnp.zeros((8, COLS), F32)
+        for m in range(HERE):
+            found += pull_apart(m, part)
+        return found
+
+    wait(shared[0])
+    loss_tile = grads_of(0)
+    over_rows(6, 4, lambda e: top(e, True))
+    tap_grads(1, range(6, 10), True)
+    backward(1, 7, None)
+    wait(shared[1])
+    loss_tile += grads_of(1)
+    for e in (4, 5, 10, 11):
+        top(e, True)
+    tap_grads(1, (4, 5, 10, 11), False)
+    core_1 = to_core(1)
+    backward(1, 5, None)
+    backward(1, 9, None)
+    wait(core_1)
+    plane_1 = to_plane(1)
     tap_grads(0, range(5, 11), True)
-    wait(edge_copies)
-    for m in range(HERE):
-        pull_apart(m, (2,), weight_tiles[1])
+    wait(shared[2])
+    grads_of(2)
     for e in (2, 3, 12, 13):
         top(e, False)
     for e in (3, 11):
         backward(1, e, None)
     tap_grads(0, (4, 11), False)
-    to_parts(0)
-    first_0 = scatter(0)
-    wait(first_1)
-    second_1 = spread_out(1)
+    core_0 = to_core(0)
 
     small[...] = jnp.zeros_like(small)
     sum_noise = tap_sum.at[0, pl.ds(0, CH), pl.ds(0, NOISE)]
@@ -539,42 +573,49 @@
     def last(e, m, entry_grad):
         sum_noise[...] += dot_rows(entry_grad, noise[e, m].astype(BF16))
 
-    over(4, 4, lambda e: backward(0, e, last))
+    over(4, 2, lambda e: backward(0, e, last))
+    wait(core_0)
+    plane_0 = to_plane(0)
+    over(8, 2, lambda e: backward(0, e, last))
     column = lax.broadcasted_iota(jnp.int32, (CH, NOISE), 1)
     late = sum_noise[...]
-    for at in range(5):
-        small[pl.ds(at, 1), pl.ds(0, CH)] = as_row(jnp.sum(sums[at], axis=1, keepdims=True))
+    rows = [as_row(jnp.sum(sums[at], axis=1, keepdims=True)) for at in range(5)]
     for k in range(NOISE):
-        picked = jnp.sum(jnp.where(column == k, late, 0.0), axis=1, keepdims=True)
-        small[pl.ds(5 + k, 1), pl.ds(0, CH)] = as_row(picked)
-    loss = jnp.sum(jnp.sum(loss_tile, axis=0, keepdims=True), axis=1, keepdims=True) * (1.0 / cells)
-    small[pl.ds(13, 1), :] = jnp.broadcast_to(loss, (1, 128))
-    small_in[in_plane] = small[...]
-    small_1 = [
-        send(small, small_in.at[in_plane], small_sems, step, device) for step, (device, _) in enumerate(plane)
-    ]
-    wait(first_0)
-    second_0 = spread_out(0)
-    wait(second_1)
-    back_1 = gather(1)
+        rows.append(as_row(jnp.sum(jnp.where(column == k, late, 0.0), axis=1, keepdims=True)))
+    loss = jnp.sum(jnp.sum(loss_tile, axis=0, keepdims=True), axis=1, keepdims=True) * (0.5 / cells)
+    rows.append(jnp.broadcast_to(loss, (1, CH)))
+    for at, row in enumerate(rows):
+        small[pl.ds(at // 2, 1), pl.ds(CH * (at % 2), CH)] = row
+    small_0 = across(small, small_core, core_sems, 4)
+    wait(plane_1)
+    depth_1 = to_depth(1)
+    wait(small_0)
+    small_in[in_plane] = small[...] + small_core[...]
+    mine = small_in.at[in_plane]
+    small_1 = [send(mine, mine, small_sems, step, device) for step, (device, _) in enumerate(plane)]
+    wait(plane_0)
+    depth_0 = to_depth(0)
+    wait(depth_1)
+    back_1 = to_plane_again(1)
     wait(small_1)
     total = small_in[0]
     for rank in range(1, GROUP):
         total = total + small_in[rank]
-    small_line[in_line] = total
-    small_2 = [
-        send(small_line.at[in_line], small_line.at[in_line], small_line_sems, step, device)
-        for step, (device, _) in enumerate(line)
-    ]
-    wait(second_0)
-    back_0 = gather(0)
+    small_line[depth] = total
+    mine = small_line.at[depth]
+    small_2 = [send(mine, mine, small_line_sems, step, device) for step, (device, _) in enumerate(line)]
+    wait(depth_0)
+    back_0 = to_plane_again(0)
     wait(back_1)
+    last_1 = to_core_again(1)
     wait(small_2)
     total = small_line[0]
-    for rank in range(1, GROUP):
+    for rank in range(1, DEPTH):
         total = total + small_line[rank]
     small_out[...] = total
     wait(back_0)
+    last_0 = to_core_again(0)
+    wait(last_1 + last_0)
 
 
 def unpack_kernel(
@@ -582,14 +623,16 @@
 ):
     pred_out[...] = predictions[...]
     for b in range(2):
-        for at in range(GROUP):
-            whole[pl.ds(CHUNK * (at // 2), CHUNK), pl.ds(128 * (at % 2), 128)] = gathered[b, at]
+        for half in range(2):
+            for at in range(GROUP):
+                whole[pl.ds(PART * (GROUP * half + at), PART), :] = gathered[b, half, at, pl.ds(0, PART), :]
         for dr in range(3):
             for dc in range(3):
                 grad_conv[b, 3 * dr + dc] = whole[pl.ds(CH * dc, CH), pl.ds(CH * dr, CH)]
     for out, first, count in ((grad_gain, 0, 2), (grad_head_gain, 2, 1), (grad_head, 3, 2), (grad_noise, 5, NOISE)):
-        out[...] = small[pl.ds(first, count), pl.ds(0, CH)]
-    loss[...] = small[pl.ds(13, 1), pl.ds(0, 1)]
+        for at in range(count):
+            out[pl.ds(at, 1), :] = small[pl.ds((first + at) // 2, 1), pl.ds(CH * ((first + at) % 2), CH)]
+    loss[...] = small[pl.ds(6, 1), pl.ds(CH, 1)]
 
 
 def on_device(
@@ -650,32 +693,35 @@
         edge_out=pltpu.VMEM((2, 8, COLS), F32),
         edge_in=pltpu.VMEM((2, 8, COLS), F32),
         target_tiles=pltpu.VMEM((3, 8, COLS), F32),
-        weight_tiles=pltpu.VMEM((2, 8, COLS), F32),
+        weight_tiles=pltpu.VMEM((3, 8, COLS), F32),
         own_pred=pltpu.VMEM((3, HERE, 8, COLS), F32),
         all_pred=pltpu.VMEM((MEMS, 3, HERE, 8, COLS), F32),
         pred_grad=pltpu.VMEM((3, HERE, 8, COLS), F32),
         sums=pltpu.VMEM((5, CH, COLS), F32),
         tap_sum=pltpu.VMEM((2, 3 * CH, 256), F32),
-        parts=pltpu.VMEM((2, GROUP, CHUNK, 128), F32),
-        scattered=pltpu.VMEM((2, GROUP - 1, CHUNK, 128), F32),
-        spread=pltpu.VMEM((2, GROUP, CHUNK, 128), F32),
-        small=pltpu.VMEM((16, 128), F32),
-        small_in=pltpu.VMEM((GROUP, 16, 128), F32),
-        small_line=pltpu.VMEM((GROUP, 16, 128), F32),
+        parts=pltpu.VMEM((2, 2, GROUP, 8, COLS), F32),
+        core_in=pltpu.VMEM((2, GROUP, 8, COLS), F32),
+        scattered=pltpu.VMEM((2, GROUP - 1, 8, COLS), F32),
+        spread=pltpu.VMEM((2, DEPTH, 8, COLS), F32),
+        small=pltpu.VMEM((8, 128), F32),
+        small_core=pltpu.VMEM((8, 128), F32),
+        small_in=pltpu.VMEM((GROUP, 8, 128), F32),
+        small_line=pltpu.VMEM((DEPTH, 8, 128), F32),
         halo_sems=sems(2, 6),
-        mem_sems=sems(2, 2, MEMS - 1),
+        mem_sems=sems(3, 2, MEMS - 1),
+        core_sems=sems(2, 5),
         plane_sems=sems(2, 2, GROUP - 1),
-        line_sems=sems(2, 2, GROUP - 1),
+        line_sems=sems(2, 2, DEPTH - 1),
         back_sems=sems(2, 2, GROUP - 1),
         small_sems=sems(2, GROUP - 1),
-        small_line_sems=sems(2, GROUP - 1),
+        small_line_sems=sems(2, DEPTH - 1),
     )
     predictions, gathered, small = pl.pallas_call(
         step_kernel,
         out_shape=(
             jax.ShapeDtypeStruct((HERE, 2, ROWS, COLS), F32),
-            jax.ShapeDtypeStruct((2, GROUP, CHUNK, 128), F32),
-            jax.ShapeDtypeStruct((16, 128), F32),
+            jax.ShapeDtypeStruct((2, 2, GROUP, 8, COLS), F32),
+            jax.ShapeDtypeStruct((8, 128), F32),
         ),
         in_specs=[far] * 9,
         out_specs=(vmem, vmem, vmem),

time: 58.5 us -> 52.6 us (0.90)
  Pallas kernels: 57.7 us -> 51.8 us
    pallas_call x1, Pallas kernels: 55.8 us -> 49.8 us  [on_device(): pl.pallas_call(step_kernel, out_shape=(jax.ShapeDtypeStruct((HERE, 2, ROW...]
where the time goes in v4:
time: 52.6 us; the launch traced here: 52.4 us
  Pallas kernels  51.8 us (98%)
  between operations  0.64 us (1%)
    pallas_call x1, Pallas kernels, on_device(): pl.pallas_call(step_kernel, out_shape=(jax.ShapeDtypeStruct((HERE, 2, ROW...  49.8 us
    pallas_call x1, Pallas kernels, on_device(): pl.pallas_call(unpack_kernel, out_shape=(jax.ShapeDtypeStruct((1, 1), F32...  2.02 us

profile of v4, /device:TPU:1, one launch (start us, length us, event | category | flops | bytes accessed | tf_op | source)
XLA Modules:
  0.0 52.4 jit_solution(2736700479987412915)
XLA Ops:
  0.6 49.8 %train_step.1 = (f32[2,2,8,256]{3,2,1,0:T(8,128)}, f32[2,2,16,8,256]{4,3,2,1,0:T(8,128)}, f32[8,128]{1,0:T(8,128)}) custom-call(bf16[2,64,8,256]{3,2,1,0:T(8,128)(2,1)} %block_input_far.1, s32[2]{0:T(128)} %seeds_far.1, f32[2,8,256]{2,1,0:T(8,128)} %targets_far.1, s32[8,256]{1,0:T(8,128)} %land_mask_far.1, bf16[8,64]{1,0:T(8,128)(2,1)} %bitcast.5, ...), custom_call_target="tpu_custom_call" | custom-call | tf_op jit(solution)/shard_map/train_step/pallas_call | solution.py:719
  50.4 2.0 %unpack.1 = (f32[1,1]{1,0:T(1,128)}, f32[2,2,8,256]{3,2,1,0:T(8,128)}, f32[2,9,64,64]{3,2,1,0:T(8,128)}, f32[2,64]{1,0:T(2,128)}, f32[2,64]{1,0:T(2,128)}, /*index=5*/f32[1,64]{1,0:T(1,128)}, f32[8,64]{1,0:T(8,128)}) custom-call(f32[2,2,8,256]{3,2,1,0:T(8,128)} %get-tuple-element.17.predictions, f32[2,2,16,8,256]{4,3,2,1,0:T(8,128)} %get-tuple-element.18.gathered, ...), custom_call_target="tpu_custom_call" | custom-call | tf_op jit(solution)/shard_map/unpack/pallas_call | solution.py:744

commit v5 on v4

--- a/solution.py
+++ b/solution.py
@@ -20,6 +20,7 @@
 EXT = ROWS + 2 * HALO
 GRID_ROWS = ROWS * TILES
 PART = 6
+DENSE = 9
 DEPTH = 8
 VMEM_BYTES = 63 * 2**20
 F32 = jnp.float32
@@ -309,7 +310,6 @@
     for at in range(5):
         sums[at] = jnp.zeros((CH, COLS), F32)
     tap_sum[...] = jnp.zeros_like(tap_sum)
-    parts[...] = jnp.zeros_like(parts)
 
     def inside(e):
         row = tile * ROWS - HALO + e
@@ -318,11 +318,13 @@
     def make_noise(e):
         row = jnp.clip(tile * ROWS - HALO + e, 0, GRID_ROWS - 1)
         for m in range(HERE):
-            noise[e, m] = noise_row(seeds[m], row).astype(F32)
+            field = noise_row(seeds[m], row)
+            noise[e, m] = field.astype(F32)
+            stream0[e, m] = dot(noise_taps[...], field)
 
     def entry(e):
         for m in range(HERE):
-            stream = raw[e, m].astype(F32) + dot(noise_taps[...], noise[e, m].astype(BF16))
+            stream = raw[e, m].astype(F32) + stream0[e, m]
             stream0[e, m] = stream
             inverse = inverse_scale(stream)
             inverse0[e, m] = jnp.broadcast_to(inverse, (8, COLS))
@@ -503,8 +505,11 @@
     def to_core(b):
         for half in range(2):
             for at in range(GROUP):
-                rows = pl.ds(PART * (GROUP * half + at), PART)
-                parts[b, half, at, pl.ds(0, PART), :] = tap_sum[b, rows, :]
+                first = PART * (GROUP * half + at)
+                parts[b, half, at, pl.ds(0, PART), :] = tap_sum[b, pl.ds(first, PART), pl.ds(0, 128)]
+                for side in range(2):
+                    rest = tap_sum[b, pl.ds(first + 3 * side, 3), pl.ds(128, CH)]
+                    parts[b, half, at, pl.ds(PART, 3), pl.ds(CH * side, CH)] = rest
         return across(parts.at[b, other_core], core_in.at[b], core_sems, b)
 
     def to_plane(b):
@@ -625,7 +630,11 @@
     for b in range(2):
         for half in range(2):
             for at in range(GROUP):
-                whole[pl.ds(PART * (GROUP * half + at), PART), :] = gathered[b, half, at, pl.ds(0, PART), :]
+                first = PART * (GROUP * half + at)
+                whole[pl.ds(first, PART), pl.ds(0, 128)] = gathered[b, half, at, pl.ds(0, PART), :]
+                for side in range(2):
+                    rest = gathered[b, half, at, pl.ds(PART, 3), pl.ds(CH * side, CH)]
+                    whole[pl.ds(first + 3 * side, 3), pl.ds(128, CH)] = rest
         for dr in range(3):
             for dc in range(3):
                 grad_conv[b, 3 * dr + dc] = whole[pl.ds(CH * dc, CH), pl.ds(CH * dr, CH)]
@@ -699,10 +708,10 @@
         pred_grad=pltpu.VMEM((3, HERE, 8, COLS), F32),
         sums=pltpu.VMEM((5, CH, COLS), F32),
         tap_sum=pltpu.VMEM((2, 3 * CH, 256), F32),
-        parts=pltpu.VMEM((2, 2, GROUP, 8, COLS), F32),
-        core_in=pltpu.VMEM((2, GROUP, 8, COLS), F32),
-        scattered=pltpu.VMEM((2, GROUP - 1, 8, COLS), F32),
-        spread=pltpu.VMEM((2, DEPTH, 8, COLS), F32),
+        parts=pltpu.VMEM((2, 2, GROUP, DENSE, 128), F32),
+        core_in=pltpu.VMEM((2, GROUP, DENSE, 128), F32),
+        scattered=pltpu.VMEM((2, GROUP - 1, DENSE, 128), F32),
+        spread=pltpu.VMEM((2, DEPTH, DENSE, 128), F32),
         small=pltpu.VMEM((8, 128), F32),
         small_core=pltpu.VMEM((8, 128), F32),
         small_in=pltpu.VMEM((GROUP, 8, 128), F32),
@@ -720,7 +729,7 @@
         step_kernel,
         out_shape=(
             jax.ShapeDtypeStruct((HERE, 2, ROWS, COLS), F32),
-            jax.ShapeDtypeStruct((2, 2, GROUP, 8, COLS), F32),
+            jax.ShapeDtypeStruct((2, 2, GROUP, DENSE, 128), F32),
             jax.ShapeDtypeStruct((8, 128), F32),
         ),
         in_specs=[far] * 9,

time: 52.6 us -> 51.9 us (0.987)
  Pallas kernels: 51.8 us -> 51.2 us
    pallas_call x1, Pallas kernels: 49.8 us -> 49.1 us  [on_device(): pl.pallas_call(step_kernel, out_shape=(jax.ShapeDtypeStruct((HERE, 2, ROW...]
where the time goes in v5:
time: 51.9 us; the launch traced here: 51.8 us
  Pallas kernels  51.2 us (99%)
  between operations  0.64 us (1%)
    pallas_call x1, Pallas kernels, on_device(): pl.pallas_call(step_kernel, out_shape=(jax.ShapeDtypeStruct((HERE, 2, ROW...  49.1 us
    pallas_call x1, Pallas kernels, on_device(): pl.pallas_call(unpack_kernel, out_shape=(jax.ShapeDtypeStruct((1, 1), F32...  2.1 us

profile of v5, /device:TPU:1, one launch (start us, length us, event | category | flops | bytes accessed | tf_op | source)
XLA Modules:
  0.0 51.8 jit_solution(440074869459041220)
XLA Ops:
  0.6 49.1 %train_step.1 = (f32[2,2,8,256]{3,2,1,0:T(8,128)}, f32[2,2,16,9,128]{4,3,2,1,0:T(8,128)}, f32[8,128]{1,0:T(8,128)}) custom-call(bf16[2,64,8,256]{3,2,1,0:T(8,128)(2,1)} %block_input_far.1, s32[2]{0:T(128)} %seeds_far.1, f32[2,8,256]{2,1,0:T(8,128)} %targets_far.1, s32[8,256]{1,0:T(8,128)} %land_mask_far.1, bf16[8,64]{1,0:T(8,128)(2,1)} %bitcast.5, ...), custom_call_target="tpu_custom_call" | custom-call | tf_op jit(solution)/shard_map/train_step/pallas_call | solution.py:728
  49.7 2.1 %unpack.1 = (f32[1,1]{1,0:T(1,128)}, f32[2,2,8,256]{3,2,1,0:T(8,128)}, f32[2,9,64,64]{3,2,1,0:T(8,128)}, f32[2,64]{1,0:T(2,128)}, f32[2,64]{1,0:T(2,128)}, /*index=5*/f32[1,64]{1,0:T(1,128)}, f32[8,64]{1,0:T(8,128)}) custom-call(f32[2,2,8,256]{3,2,1,0:T(8,128)} %get-tuple-element.17.predictions, f32[2,2,16,9,128]{4,3,2,1,0:T(8,128)} %get-tuple-element.18.gathered, ...), custom_call_target="tpu_custom_call" | custom-call | tf_op jit(solution)/shard_map/unpack/pallas_call | solution.py:753

commit v6 on v5

--- a/solution.py
+++ b/solution.py
@@ -477,7 +477,8 @@
                 windows.append(inputs[pl.ds(e - 1, 3), m].reshape(3 * CH, COLS))
         found = dot_rows(jnp.concatenate(shifted, axis=1), jnp.concatenate(windows, axis=1))
         at = pl.ds(0, 3 * CH)
-        tap_sum[b, :, at] = found if fresh else tap_sum[b, :, at] + found
+        rows_here = pl.ds(0, 3 * CH)
+        tap_sum[b, rows_here, at] = found if fresh else tap_sum[b, rows_here, at] + found
 
     def backward(b, e, last):
         source, stream, inverses = ((grads0, stream0, inverse0), (grads1, stream1, inverse1))[b]
@@ -707,8 +708,8 @@
         all_pred=pltpu.VMEM((MEMS, 3, HERE, 8, COLS), F32),
         pred_grad=pltpu.VMEM((3, HERE, 8, COLS), F32),
         sums=pltpu.VMEM((5, CH, COLS), F32),
-        tap_sum=pltpu.VMEM((2, 3 * CH, 256), F32),
-        parts=pltpu.VMEM((2, 2, GROUP, DENSE, 128), F32),
+        tap_sum=pltpu.VMEM((2, 3 * CH + 8, 256), F32),
+        parts=pltpu.VMEM((3, 2, GROUP, DENSE, 128), F32),
         core_in=pltpu.VMEM((2, GROUP, DENSE, 128), F32),
         scattered=pltpu.VMEM((2, GROUP - 1, DENSE, 128), F32),
         spread=pltpu.VMEM((2, DEPTH, DENSE, 128), F32),
@@ -763,7 +764,7 @@
         ),
         in_specs=[vmem] * 3,
         out_specs=(vmem,) * 7,
-        scratch_shapes=[pltpu.VMEM((3 * CH, 256), F32)],
+        scratch_shapes=[pltpu.VMEM((3 * CH + 8, 256), F32)],
         compiler_params=pltpu.CompilerParams(vmem_limit_bytes=VMEM_BYTES),
         name="unpack",
     )(predictions, gathered, small)

time: 51.9 us -> 51.9 us (level)
  no operation moved by 1% of the time
where the time goes in v6:
time: 51.9 us; the launch traced here: 51.8 us
  Pallas kernels  51.2 us (99%)
  between operations  0.64 us (1%)
    pallas_call x1, Pallas kernels, on_device(): pl.pallas_call(step_kernel, out_shape=(jax.ShapeDtypeStruct((HERE, 2, ROW...  49.1 us
    pallas_call x1, Pallas kernels, on_device(): pl.pallas_call(unpack_kernel, out_shape=(jax.ShapeDtypeStruct((1, 1), F32...  2.1 us

profile of v6, /device:TPU:1, one launch (start us, length us, event | category | flops | bytes accessed | tf_op | source)
XLA Modules:
  0.0 51.8 jit_solution(15684820177640820213)
XLA Ops:
  0.6 49.1 %train_step.1 = (f32[2,2,8,256]{3,2,1,0:T(8,128)}, f32[2,2,16,9,128]{4,3,2,1,0:T(8,128)}, f32[8,128]{1,0:T(8,128)}) custom-call(bf16[2,64,8,256]{3,2,1,0:T(8,128)(2,1)} %block_input_far.1, s32[2]{0:T(128)} %seeds_far.1, f32[2,8,256]{2,1,0:T(8,128)} %targets_far.1, s32[8,256]{1,0:T(8,128)} %land_mask_far.1, bf16[8,64]{1,0:T(8,128)(2,1)} %bitcast.5, ...), custom_call_target="tpu_custom_call" | custom-call | tf_op jit(solution)/shard_map/train_step/pallas_call | solution.py:729
  49.7 2.1 %unpack.1 = (f32[1,1]{1,0:T(1,128)}, f32[2,2,8,256]{3,2,1,0:T(8,128)}, f32[2,9,64,64]{3,2,1,0:T(8,128)}, f32[2,64]{1,0:T(2,128)}, f32[2,64]{1,0:T(2,128)}, /*index=5*/f32[1,64]{1,0:T(1,128)}, f32[8,64]{1,0:T(8,128)}) custom-call(f32[2,2,8,256]{3,2,1,0:T(8,128)} %get-tuple-element.17.predictions, f32[2,2,16,9,128]{4,3,2,1,0:T(8,128)} %get-tuple-element.18.gathered, ...), custom_call_target="tpu_custom_call" | custom-call | tf_op jit(solution)/shard_map/unpack/pallas_call | solution.py:754
